TPU v7x, 512 devices: a whole 4x8x8 slice. The times are simulated.
512 devices in a mesh: blk: 16 (over x, z_hi), sub: 32 (over y, z_lo, core).
Axes of the slice: x: 4, y: 8, z: 8 (z_hi: 4, z_lo: 2; z = z_hi * 2 + z_lo), core: 2. Of those that a mesh axis runs over, the one named last changes fastest.
Arguments:
- green: bfloat16 [2, 2, 6, 65536, 512], P(None, None, None, ('blk', 'sub')), may hold values from -6 to 6
- mechanism: float32 [6, 65536], P(None, ('blk', 'sub')), may hold values from -0.009765625 to 0.009765625
- slip: bfloat16 [128, 65536], P(None, ('blk', 'sub')), may hold values from 0.099609375 to 3
- onset: int32 [8, 65536], P(None, ('blk', 'sub')), may hold values from 0 to 1023
- pattern_of_variation: int32 [512], replicated, may hold values from 0 to 127
- hypo_of_variation: int32 [512], replicated, may hold values from 0 to 7
Outputs:
- seismograms: float32 [512, 2, 1024], P(('blk', 'sub'))
All inputs are finite; a program needn't handle non-finite values.
Results may differ from a plain program's by a relative error of at most 0.0029.
Values may be sent and summed in bfloat16 or wider, within the bound.
No kernel may reach another device: no remote copies, remote signals or barrier semaphores. Data moves between devices by JAX's collectives and lax.ppermute only.
A program may use at most 64 MiB of HBM per device.

v0:
```python
import math

import jax
import jax.numpy as jnp
from jax import lax
from jax.sharding import PartitionSpec as P


def shifted_2(block, axis, distance):
    devices = range(lax.axis_size(axis))
    route = [((i - distance) % len(devices), i) for i in devices]
    return lax.ppermute(block, axis, route)


def inverse_table(freq_count, samples):
    freq = jnp.arange(freq_count, dtype=jnp.int32)
    times = jnp.arange(samples, dtype=jnp.int32)
    steps = freq[:, None] * times[None, :] % samples
    angle = steps.astype(jnp.float32) * (2.0 * math.pi / samples)
    weight = jnp.where(freq == 0, 0.5, 1.0).astype(jnp.float32) / math.sqrt(freq_count)
    return jnp.concatenate(
        [weight[:, None] * jnp.cos(angle), -weight[:, None] * jnp.sin(angle)], axis=0
    )


def build_table(merged, slip, onset, freq, samples):
    real_part = jnp.transpose(merged[0], (1, 0, 2))
    imag_part = jnp.transpose(merged[1], (1, 0, 2))
    steps = onset[:, :, None] * freq[None, None, :] % samples
    angle = steps.astype(jnp.float32) * (2.0 * math.pi / samples)
    cosine = jnp.cos(angle)[:, :, None, :]
    sine = jnp.sin(angle)[:, :, None, :]
    shifted_re = cosine * real_part[None] + sine * imag_part[None]
    shifted_im = cosine * imag_part[None] - sine * real_part[None]
    shifted = jnp.stack([shifted_re, shifted_im], axis=3).astype(jnp.bfloat16)
    shifted = shifted.reshape(shifted.shape[0], shifted.shape[1], -1)
    table = jnp.einsum("ps,hsx->hpx", slip, shifted, preferred_element_type=jnp.float32)
    return table.reshape(-1, table.shape[2])


def on_device(green, mechanism, slip, onset, pattern_of_variation, hypo_of_variation):
    freq_count = green.shape[4]
    samples = 2 * freq_count
    comps = green.shape[1]
    merged = jnp.sum(mechanism[None, None, :, :, None] * green.astype(jnp.float32), axis=2)
    combos = hypo_of_variation * slip.shape[0] + pattern_of_variation
    blocks = lax.axis_size("blk")
    mine = lax.axis_index("blk")
    block_rows = combos.shape[0] // blocks

    def block_ids(block):
        return lax.dynamic_slice_in_dim(combos, block * block_rows, block_rows)

    freq = jnp.arange(freq_count, dtype=jnp.int32)
    table = build_table(merged, slip, onset, freq, samples)
    width = table.shape[1]

    def forward_step(turn, carried):
        arrived = shifted_2(carried, "blk", 1)
        block = (mine - turn - 1) % blocks
        return arrived + jnp.take(table, block_ids(block), axis=0)

    summed = lax.fori_loop(0, blocks, forward_step, jnp.zeros((block_rows, width), jnp.float32))
    spectra = lax.psum_scatter(summed, "sub", scatter_dimension=0, tiled=True)
    count = spectra.shape[0]
    rows = spectra.reshape(count * comps, 2 * freq_count)
    result = jnp.dot(
        rows,
        inverse_table(freq_count, samples),
        precision=lax.Precision.HIGHEST,
        preferred_element_type=jnp.float32,
    )
    return result.reshape(count, comps, samples)


def solution(mesh):
    in_specs = (
        P(None, None, None, ("blk", "sub"), None),
        P(None, ("blk", "sub")),
        P(None, ("blk", "sub")),
        P(None, ("blk", "sub")),
        P(),
        P(),
    )
    out_specs = P(("blk", "sub"), None, None)
    return jax.shard_map(
        on_device, mesh=mesh, in_specs=in_specs, out_specs=out_specs, check_vma=False
    )
```

profile of v0, /device:TPU:1, one launch (start us, length us, event | category | flops | bytes accessed | tf_op | source)
XLA Modules:
  0.0 584.5 jit_solution(10457958905919421912)
XLA Ops:
  6.6 9.1 %fusion.20 = (f32[8,128,512]{2,1,0:T(8,128)S(1)}, f32[8,128,512]{2,1,0:T(8,128)S(1)}) fusion(s32[8,128]{1,0:T(8,128)} %param.11), kind=kLoop, calls=%fused_computation.36 | loop fusion | flops 7340032 | bytes 4198400 | tf_op jit(solution)/shard_map/cos | solution.py:31
  15.7 0.7 multiply_reduce_fusion
  16.5 0.4 copy.7
  16.9 0.4 copy.8
  17.3 9.0 %add_convert_fusion = (bf16[8,128,2,1,512]{4,3,2,1,0:T(2,128)(2,1)S(1)}, bf16[8,128,2,1,512]{4,3,2,1,0:T(2,128)(2,1)S(1)}) fusion(f32[128,2,512]{2,1,0:T(2,128)S(1)} %copy.8, f32[8,128,512]{2,1,0:T(8,128)S(1)} %get-tuple-element.175, f32[128,2,512]{2,1,0:T(2,128)S(1)} %copy.7, f32[8,128,512]{2,1,0:T(8,128)S(1)} %get-tuple-element.174), kind=kLoop, calls=%fused_computation.13 | loop fusion | flops 8388608 | bytes 9437184 | tf_op jit(solution)/shard_map/convert
  26.2 10.5 %pad_maximum_fusion = bf16[8,128,2,2,512]{4,3,2,1,0:T(2,128)(2,1)} fusion(bf16[8,128,2,1,512]{4,3,2,1,0:T(2,128)(2,1)S(1)} %get-tuple-element.171, bf16[8,128,2,1,512]{4,3,2,1,0:T(2,128)(2,1)S(1)} %get-tuple-element.170), kind=kLoop, calls=%fused_computation.7 | loop fusion | flops 8388608 | bytes 8388608 | tf_op jit(solution)/shard_map/stack | solution.py:35
  36.7 7.8 %convert_element_type.25 = bf16[8,128,2048]{2,1,0:T(8,128)(2,1)} reshape(bf16[8,128,2,2,512]{4,3,2,1,0:T(2,128)(2,1)} %pad_maximum_fusion) | data formatting | bytes 8388608 | tf_op jit(solution)/shard_map/convert_element_type | solution.py:35
  44.6 6.7 %fusion.21 = f32[8,2048,128]{1,2,0:T(8,128)} fusion(bf16[8,128,2048]{2,1,0:T(8,128)(2,1)} %convert_element_type.25, bf16[128,128]{1,0:T(8,128)(2,1)S(1)} %copy-done), kind=kOutput, calls=%fused_computation.39 | convolution fusion | flops 536870912 | bytes 12615680 | tf_op jit(solution)/shard_map/ps,hsx->hpx/dot_general | solution.py:37
  51.3 249.0 %while.16 = (s32[]{:T(128)}, f32[32,2048]{1,0:T(8,128)S(1)}, s32[]{:T(128)}, s32[512]{0:T(512)S(1)}, f32[1024,2048]{1,0:T(8,128)}, /*index=5*/s32[]{:T(128)}, s3...) while((s32[]{:T(128)}, f32[32,2048]{1,0:T(8,128)S(1)}, s32[]{:T(128)}, ...), condition=%wide.region_2.3_spmd.clone, body=%wide.region_1.2_spmd.clone.sunk | while | flops 197844 | bytes 2888606 | solution.py:63
  51.3 6.6 %collective-permute-start = (f32[32,2048]{1,0:T(8,128)S(1)}, f32[32,2048]{1,0:T(8,128)S(1)}, u32[]{:S(2)}, u32[]{:S(2)}) collective-permute-start(f32[32,2048]{1,0:T(8,128)S(1)} %broadcast_select_fusion.2), channel_id=1, source_target_pairs={{480,0},{0,32},{32,64},{64,96},{96,128},{128,160},{160,192},{192,2... | collective-permute-start | bytes 786440 | tf_op jit(solution)/shard_map/while/body/eval_jaxpr/ppermute | solution.py:12
  58.1 4.1 gather_fusion
  62.3 8.5 %collective-permute-done = f32[32,2048]{1,0:T(8,128)S(1)} collective-permute-done((f32[32,2048]{1,0:T(8,128)S(1)}, f32[32,2048]{1,0:T(8,128)S(1)}, u32[]{:S(2)}, u32[]{:S(2)}) %collective-permute-start) | collective-permute-done | bytes 262176 | tf_op jit(solution)/shard_map/while/body/eval_jaxpr/ppermute | solution.py:12
  70.9 4.8 collective-permute-start
  75.8 4.1 gather_fusion
  80.0 8.4 %collective-permute-done = f32[32,2048]{1,0:T(8,128)S(1)} collective-permute-done((f32[32,2048]{1,0:T(8,128)S(1)}, f32[32,2048]{1,0:T(8,128)S(1)}, u32[]{:S(2)}, u32[]{:S(2)}) %collective-permute-start) | collective-permute-done | bytes 262176 | tf_op jit(solution)/shard_map/while/body/eval_jaxpr/ppermute | solution.py:12
  88.5 1.9 collective-permute-start
  90.6 4.1 gather_fusion
  94.7 10.9 %collective-permute-done = f32[32,2048]{1,0:T(8,128)S(1)} collective-permute-done((f32[32,2048]{1,0:T(8,128)S(1)}, f32[32,2048]{1,0:T(8,128)S(1)}, u32[]{:S(2)}, u32[]{:S(2)}) %collective-permute-start) | collective-permute-done | bytes 262176 | tf_op jit(solution)/shard_map/while/body/eval_jaxpr/ppermute | solution.py:12
  105.6 0.1 select_add_fusion.2
  105.8 1.9 collective-permute-start
  107.8 4.1 gather_fusion
  112.0 5.2 collective-permute-done
  117.3 1.9 collective-permute-start
  119.3 4.1 gather_fusion
  123.5 7.3 %collective-permute-done = f32[32,2048]{1,0:T(8,128)S(1)} collective-permute-done((f32[32,2048]{1,0:T(8,128)S(1)}, f32[32,2048]{1,0:T(8,128)S(1)}, u32[]{:S(2)}, u32[]{:S(2)}) %collective-permute-start) | collective-permute-done | bytes 262176 | tf_op jit(solution)/shard_map/while/body/eval_jaxpr/ppermute | solution.py:12
  130.9 1.9 collective-permute-start
  132.9 4.1 gather_fusion
  137.1 7.2 %collective-permute-done = f32[32,2048]{1,0:T(8,128)S(1)} collective-permute-done((f32[32,2048]{1,0:T(8,128)S(1)}, f32[32,2048]{1,0:T(8,128)S(1)}, u32[]{:S(2)}, u32[]{:S(2)}) %collective-permute-start) | collective-permute-done | bytes 262176 | tf_op jit(solution)/shard_map/while/body/eval_jaxpr/ppermute | solution.py:12
  144.4 1.9 collective-permute-start
  146.4 4.1 gather_fusion
  150.6 12.3 %collective-permute-done = f32[32,2048]{1,0:T(8,128)S(1)} collective-permute-done((f32[32,2048]{1,0:T(8,128)S(1)}, f32[32,2048]{1,0:T(8,128)S(1)}, u32[]{:S(2)}, u32[]{:S(2)}) %collective-permute-start) | collective-permute-done | bytes 262176 | tf_op jit(solution)/shard_map/while/body/eval_jaxpr/ppermute | solution.py:12
  163.0 1.9 collective-permute-start
  165.0 4.1 gather_fusion
  169.2 11.4 %collective-permute-done = f32[32,2048]{1,0:T(8,128)S(1)} collective-permute-done((f32[32,2048]{1,0:T(8,128)S(1)}, f32[32,2048]{1,0:T(8,128)S(1)}, u32[]{:S(2)}, u32[]{:S(2)}) %collective-permute-start) | collective-permute-done | bytes 262176 | tf_op jit(solution)/shard_map/while/body/eval_jaxpr/ppermute | solution.py:12
  180.7 1.9 collective-permute-start
  182.7 4.1 gather_fusion
  186.9 7.4 %collective-permute-done = f32[32,2048]{1,0:T(8,128)S(1)} collective-permute-done((f32[32,2048]{1,0:T(8,128)S(1)}, f32[32,2048]{1,0:T(8,128)S(1)}, u32[]{:S(2)}, u32[]{:S(2)}) %collective-permute-start) | collective-permute-done | bytes 262176 | tf_op jit(solution)/shard_map/while/body/eval_jaxpr/ppermute | solution.py:12
  194.4 1.9 collective-permute-start
  196.5 4.1 gather_fusion
  200.6 7.6 %collective-permute-done = f32[32,2048]{1,0:T(8,128)S(1)} collective-permute-done((f32[32,2048]{1,0:T(8,128)S(1)}, f32[32,2048]{1,0:T(8,128)S(1)}, u32[]{:S(2)}, u32[]{:S(2)}) %collective-permute-start) | collective-permute-done | bytes 262176 | tf_op jit(solution)/shard_map/while/body/eval_jaxpr/ppermute | solution.py:12
  208.4 1.9 collective-permute-start
  210.4 4.1 gather_fusion
  214.6 5.1 collective-permute-done
  219.9 4.7 collective-permute-start
  224.7 4.1 gather_fusion
  228.9 5.0 collective-permute-done
  234.0 1.9 collective-permute-start
  236.0 4.1 gather_fusion
  240.2 10.1 %collective-permute-done = f32[32,2048]{1,0:T(8,128)S(1)} collective-permute-done((f32[32,2048]{1,0:T(8,128)S(1)}, f32[32,2048]{1,0:T(8,128)S(1)}, u32[]{:S(2)}, u32[]{:S(2)}) %collective-permute-start) | collective-permute-done | bytes 262176 | tf_op jit(solution)/shard_map/while/body/eval_jaxpr/ppermute | solution.py:12
  250.5 1.9 collective-permute-start
  252.5 4.1 gather_fusion
  256.7 11.9 %collective-permute-done = f32[32,2048]{1,0:T(8,128)S(1)} collective-permute-done((f32[32,2048]{1,0:T(8,128)S(1)}, f32[32,2048]{1,0:T(8,128)S(1)}, u32[]{:S(2)}, u32[]{:S(2)}) %collective-permute-start) | collective-permute-done | bytes 262176 | tf_op jit(solution)/shard_map/while/body/eval_jaxpr/ppermute | solution.py:12
  268.8 1.9 collective-permute-start
  270.8 4.1 gather_fusion
  275.0 12.6 %collective-permute-done = f32[32,2048]{1,0:T(8,128)S(1)} collective-permute-done((f32[32,2048]{1,0:T(8,128)S(1)}, f32[32,2048]{1,0:T(8,128)S(1)}, u32[]{:S(2)}, u32[]{:S(2)}) %collective-permute-start) | collective-permute-done | bytes 262176 | tf_op jit(solution)/shard_map/while/body/eval_jaxpr/ppermute | solution.py:12
  287.7 1.9 collective-permute-start
  289.7 4.1 gather_fusion
  293.9 6.3 %collective-permute-done = f32[32,2048]{1,0:T(8,128)S(1)} collective-permute-done((f32[32,2048]{1,0:T(8,128)S(1)}, f32[32,2048]{1,0:T(8,128)S(1)}, u32[]{:S(2)}, u32[]{:S(2)}) %collective-permute-start) | collective-permute-done | bytes 262176 | tf_op jit(solution)/shard_map/while/body/eval_jaxpr/ppermute | solution.py:12
  300.3 0.7 copy-done.1
  301.1 1.3 dynamic-slice
  302.3 9.2 %sine_multiply_fusion = (f32[512,1024]{1,0:T(8,128)S(1)}, f32[512,1024]{1,0:T(8,128)}) fusion(f32[512]{0:T(512)S(1)} %fusion.23, f32[512]{0:T(512)S(1)} %select_multiply_fusion), kind=kLoop, calls=%fused_computation.26 | loop fusion | flops 8388608 | bytes 4198400 | tf_op jit(solution)/shard_map/mul | solution.py:22
  311.5 260.3 %all-reduce.3.cloned.1.call-done = f32[32,2048]{1,0:T(8,128)} async-done(((f32[32,2048]{1,0:T(8,128)}), f32[32,2048]{1,0:T(8,128)}) %all-reduce.3.cloned.1.call-update) | async-done | bytes 262160
  571.8 1.5 dynamic-slice_reduce_fusion
  573.4 4.3 fusion.16
  (82 shorter events, 3.3 us)
Async XLA Ops:
  6.5 38.0 %copy-start = (bf16[128,128]{1,0:T(8,128)(2,1)S(1)}, bf16[128,128]{1,0:T(8,128)(2,1)}, u32[]{:S(2)}) copy-start(bf16[128,128]{1,0:T(8,128)(2,1)} %param.10) | copy-start | bytes 98308
  6.5 565.3 %all-reduce.3.cloned.1.call-start = ((), (), s32[]{:S(2)}) async-start(), calls=%async_computation | async-start | bytes 524288
  6.5 9.1 %copy-start.2 = (bf16[2,2,6,128,512]{4,3,2,1,0:T(8,128)(2,1)S(1)}, bf16[2,2,6,128,512]{4,3,2,1,0:T(8,128)(2,1)}, u32[]{:S(2)}) copy-start(bf16[2,2,6,128,512]{4,3,2,1,0:T(8,128)(2,1)} %param.8) | copy-start | bytes 9437188
  6.5 9.1 %copy-start.3 = (f32[6,128]{1,0:T(8,128)S(1)}, f32[6,128]{1,0:T(8,128)}, u32[]{:S(2)}) copy-start(f32[6,128]{1,0:T(8,128)} %param.9) | copy-start | bytes 9220
  44.6 6.7 %copy-start.4 = (s32[512]{0:T(512)S(1)}, s32[512]{0:T(512)}, u32[]{:S(2)}) copy-start(s32[512]{0:T(512)} %param.12) | copy-start | bytes 6148
  44.6 6.7 %copy-start.5 = (s32[512]{0:T(512)S(1)}, s32[512]{0:T(512)}, u32[]{:S(2)}) copy-start(s32[512]{0:T(512)} %param.13) | copy-start | bytes 6148
  51.3 19.4 %collective-permute-start = (f32[32,2048]{1,0:T(8,128)S(1)}, f32[32,2048]{1,0:T(8,128)S(1)}, u32[]{:S(2)}, u32[]{:S(2)}) collective-permute-start(f32[32,2048]{1,0:T(8,128)S(1)} %broadcast_select_fusion.2), channel_id=1, source_target_pairs={{480,0},{0,32},{32,64},{64,96},{96,128},{128,160},{160,192},{192,2... | collective-permute-start | bytes 786440 | tf_op jit(solution)/shard_map/while/body/eval_jaxpr/ppermute | solution.py:12
  70.9 17.5 %collective-permute-start = (f32[32,2048]{1,0:T(8,128)S(1)}, f32[32,2048]{1,0:T(8,128)S(1)}, u32[]{:S(2)}, u32[]{:S(2)}) collective-permute-start(f32[32,2048]{1,0:T(8,128)S(1)} %broadcast_select_fusion.2), channel_id=1, source_target_pairs={{480,0},{0,32},{32,64},{64,96},{96,128},{128,160},{160,192},{192,2... | collective-permute-start | bytes 786440 | tf_op jit(solution)/shard_map/while/body/eval_jaxpr/ppermute | solution.py:12
  88.5 17.1 %collective-permute-start = (f32[32,2048]{1,0:T(8,128)S(1)}, f32[32,2048]{1,0:T(8,128)S(1)}, u32[]{:S(2)}, u32[]{:S(2)}) collective-permute-start(f32[32,2048]{1,0:T(8,128)S(1)} %broadcast_select_fusion.2), channel_id=1, source_target_pairs={{480,0},{0,32},{32,64},{64,96},{96,128},{128,160},{160,192},{192,2... | collective-permute-start | bytes 786440 | tf_op jit(solution)/shard_map/while/body/eval_jaxpr/ppermute | solution.py:12
  105.8 11.4 %collective-permute-start = (f32[32,2048]{1,0:T(8,128)S(1)}, f32[32,2048]{1,0:T(8,128)S(1)}, u32[]{:S(2)}, u32[]{:S(2)}) collective-permute-start(f32[32,2048]{1,0:T(8,128)S(1)} %broadcast_select_fusion.2), channel_id=1, source_target_pairs={{480,0},{0,32},{32,64},{64,96},{96,128},{128,160},{160,192},{192,2... | collective-permute-start | bytes 786440 | tf_op jit(solution)/shard_map/while/body/eval_jaxpr/ppermute | solution.py:12
  117.3 13.4 %collective-permute-start = (f32[32,2048]{1,0:T(8,128)S(1)}, f32[32,2048]{1,0:T(8,128)S(1)}, u32[]{:S(2)}, u32[]{:S(2)}) collective-permute-start(f32[32,2048]{1,0:T(8,128)S(1)} %broadcast_select_fusion.2), channel_id=1, source_target_pairs={{480,0},{0,32},{32,64},{64,96},{96,128},{128,160},{160,192},{192,2... | collective-permute-start | bytes 786440 | tf_op jit(solution)/shard_map/while/body/eval_jaxpr/ppermute | solution.py:12
  130.9 13.4 %collective-permute-start = (f32[32,2048]{1,0:T(8,128)S(1)}, f32[32,2048]{1,0:T(8,128)S(1)}, u32[]{:S(2)}, u32[]{:S(2)}) collective-permute-start(f32[32,2048]{1,0:T(8,128)S(1)} %broadcast_select_fusion.2), channel_id=1, source_target_pairs={{480,0},{0,32},{32,64},{64,96},{96,128},{128,160},{160,192},{192,2... | collective-permute-start | bytes 786440 | tf_op jit(solution)/shard_map/while/body/eval_jaxpr/ppermute | solution.py:12
  144.4 18.5 %collective-permute-start = (f32[32,2048]{1,0:T(8,128)S(1)}, f32[32,2048]{1,0:T(8,128)S(1)}, u32[]{:S(2)}, u32[]{:S(2)}) collective-permute-start(f32[32,2048]{1,0:T(8,128)S(1)} %broadcast_select_fusion.2), channel_id=1, source_target_pairs={{480,0},{0,32},{32,64},{64,96},{96,128},{128,160},{160,192},{192,2... | collective-permute-start | bytes 786440 | tf_op jit(solution)/shard_map/while/body/eval_jaxpr/ppermute | solution.py:12
  163.0 17.6 %collective-permute-start = (f32[32,2048]{1,0:T(8,128)S(1)}, f32[32,2048]{1,0:T(8,128)S(1)}, u32[]{:S(2)}, u32[]{:S(2)}) collective-permute-start(f32[32,2048]{1,0:T(8,128)S(1)} %broadcast_select_fusion.2), channel_id=1, source_target_pairs={{480,0},{0,32},{32,64},{64,96},{96,128},{128,160},{160,192},{192,2... | collective-permute-start | bytes 786440 | tf_op jit(solution)/shard_map/while/body/eval_jaxpr/ppermute | solution.py:12
  180.7 13.6 %collective-permute-start = (f32[32,2048]{1,0:T(8,128)S(1)}, f32[32,2048]{1,0:T(8,128)S(1)}, u32[]{:S(2)}, u32[]{:S(2)}) collective-permute-start(f32[32,2048]{1,0:T(8,128)S(1)} %broadcast_select_fusion.2), channel_id=1, source_target_pairs={{480,0},{0,32},{32,64},{64,96},{96,128},{128,160},{160,192},{192,2... | collective-permute-start | bytes 786440 | tf_op jit(solution)/shard_map/while/body/eval_jaxpr/ppermute | solution.py:12
  194.4 13.8 %collective-permute-start = (f32[32,2048]{1,0:T(8,128)S(1)}, f32[32,2048]{1,0:T(8,128)S(1)}, u32[]{:S(2)}, u32[]{:S(2)}) collective-permute-start(f32[32,2048]{1,0:T(8,128)S(1)} %broadcast_select_fusion.2), channel_id=1, source_target_pairs={{480,0},{0,32},{32,64},{64,96},{96,128},{128,160},{160,192},{192,2... | collective-permute-start | bytes 786440 | tf_op jit(solution)/shard_map/while/body/eval_jaxpr/ppermute | solution.py:12
  208.4 11.3 %collective-permute-start = (f32[32,2048]{1,0:T(8,128)S(1)}, f32[32,2048]{1,0:T(8,128)S(1)}, u32[]{:S(2)}, u32[]{:S(2)}) collective-permute-start(f32[32,2048]{1,0:T(8,128)S(1)} %broadcast_select_fusion.2), channel_id=1, source_target_pairs={{480,0},{0,32},{32,64},{64,96},{96,128},{128,160},{160,192},{192,2... | collective-permute-start | bytes 786440 | tf_op jit(solution)/shard_map/while/body/eval_jaxpr/ppermute | solution.py:12
  219.9 14.0 %collective-permute-start = (f32[32,2048]{1,0:T(8,128)S(1)}, f32[32,2048]{1,0:T(8,128)S(1)}, u32[]{:S(2)}, u32[]{:S(2)}) collective-permute-start(f32[32,2048]{1,0:T(8,128)S(1)} %broadcast_select_fusion.2), channel_id=1, source_target_pairs={{480,0},{0,32},{32,64},{64,96},{96,128},{128,160},{160,192},{192,2... | collective-permute-start | bytes 786440 | tf_op jit(solution)/shard_map/while/body/eval_jaxpr/ppermute | solution.py:12
  234.0 16.3 %collective-permute-start = (f32[32,2048]{1,0:T(8,128)S(1)}, f32[32,2048]{1,0:T(8,128)S(1)}, u32[]{:S(2)}, u32[]{:S(2)}) collective-permute-start(f32[32,2048]{1,0:T(8,128)S(1)} %broadcast_select_fusion.2), channel_id=1, source_target_pairs={{480,0},{0,32},{32,64},{64,96},{96,128},{128,160},{160,192},{192,2... | collective-permute-start | bytes 786440 | tf_op jit(solution)/shard_map/while/body/eval_jaxpr/ppermute | solution.py:12
  250.5 18.1 %collective-permute-start = (f32[32,2048]{1,0:T(8,128)S(1)}, f32[32,2048]{1,0:T(8,128)S(1)}, u32[]{:S(2)}, u32[]{:S(2)}) collective-permute-start(f32[32,2048]{1,0:T(8,128)S(1)} %broadcast_select_fusion.2), channel_id=1, source_target_pairs={{480,0},{0,32},{32,64},{64,96},{96,128},{128,160},{160,192},{192,2... | collective-permute-start | bytes 786440 | tf_op jit(solution)/shard_map/while/body/eval_jaxpr/ppermute | solution.py:12
  268.8 18.8 %collective-permute-start = (f32[32,2048]{1,0:T(8,128)S(1)}, f32[32,2048]{1,0:T(8,128)S(1)}, u32[]{:S(2)}, u32[]{:S(2)}) collective-permute-start(f32[32,2048]{1,0:T(8,128)S(1)} %broadcast_select_fusion.2), channel_id=1, source_target_pairs={{480,0},{0,32},{32,64},{64,96},{96,128},{128,160},{160,192},{192,2... | collective-permute-start | bytes 786440 | tf_op jit(solution)/shard_map/while/body/eval_jaxpr/ppermute | solution.py:12
  287.7 12.5 %collective-permute-start = (f32[32,2048]{1,0:T(8,128)S(1)}, f32[32,2048]{1,0:T(8,128)S(1)}, u32[]{:S(2)}, u32[]{:S(2)}) collective-permute-start(f32[32,2048]{1,0:T(8,128)S(1)} %broadcast_select_fusion.2), channel_id=1, source_target_pairs={{480,0},{0,32},{32,64},{64,96},{96,128},{128,160},{160,192},{192,2... | collective-permute-start | bytes 786440 | tf_op jit(solution)/shard_map/while/body/eval_jaxpr/ppermute | solution.py:12
  300.3 0.7 copy-start.1
Sparse Core Ops, SparseCore 0:
  301.1 270.6 all-reduce.2
where the time goes:
time: 586 us; the launch traced here: 584 us
  waiting for transfers between devices  398 us (68%)
  local copies, waits for them, and re-layouts  78.6 us (13%)
  other arithmetic  41.7 us (7%)
  starting transfers between devices  41.1 us (7%)
  between operations  13.5 us (2%)
  matrix products  11 us (2%)
    unnamed x2, waiting for transfers between devices  260 us
    ppermute x16, waiting for transfers between devices, shifted_2(): return lax.ppermute(block, axis, route)  137 us
    gather x16, local copies, waits for them, and re-layouts, forward_step(): return arrived + jnp.take(table, block_ids(block), axis=0)  66.4 us
    ppermute x16, starting transfers between devices, shifted_2(): return lax.ppermute(block, axis, route)  41.1 us
  transfers between devices with their start and end apart: 17, of which 17 were waited for; matrix products, arithmetic and copies ran while one was open for 13% of the time, Pallas kernels for 0%

commit v1 on v0

v1 whole, which is shorter than its diff:
```python
import math

import jax
import jax.numpy as jnp
import numpy as np
from jax import lax
from jax.experimental import pallas as pl
from jax.experimental.pallas import tpu as pltpu
from jax.sharding import Mesh
from jax.sharding import PartitionSpec as P

AXES = ("x", "zh", "y", "zl", "c")
GROUP = ("x", "c")
PLANE = ("zh", "y", "zl")
CODE_TOP = 32000.0
SLIP_UNIT = 2048.0
LEAST = 4e-34
F32, BF16, I32, I16 = jnp.float32, jnp.bfloat16, jnp.int32, jnp.int16
VMEM = 48 * 1024 * 1024


def cos_sin(steps, samples):
    eighth = samples // 8
    quadrant = (steps + eighth) >> int(math.log2(samples // 4))
    rest = steps - quadrant * (samples // 4)
    t = rest.astype(F32) * (2.0 * math.pi / samples)
    t2 = t * t
    sine = t + t * t2 * (-1.0 / 6 + t2 * (1.0 / 120 + t2 * (-1.0 / 5040 + t2 * (1.0 / 362880))))
    cosine = 1.0 + t2 * (-0.5 + t2 * (1.0 / 24 + t2 * (-1.0 / 720 + t2 * (1.0 / 40320))))
    odd = (quadrant & 1) == 1
    c = jnp.where(odd, sine, cosine)
    s = jnp.where(odd, cosine, sine)
    c = jnp.where(((quadrant + 1) & 2) == 2, -c, c)
    s = jnp.where((quadrant & 2) == 2, -s, s)
    return c, s


def merge_kernel(groups, green_ref, mech_ref, slip_ref, onset_ref, msg_ref, cols, merged, top):
    step = pl.program_id(0) * pl.num_programs(1) + pl.program_id(1)
    kinds, subs, freqs = green_ref.shape[2:]
    share = freqs // groups

    @pl.when(step == 0)
    def _():
        for k in range(kinds):
            cols[k] = jnp.broadcast_to(mech_ref[k : k + 1, :], (subs, subs)).T
        top[...] = jnp.zeros_like(top)

    for tile in range(freqs // subs):
        lanes = pl.ds(tile * subs, subs)
        total = cols[0] * green_ref[0, 0, 0, :, lanes].astype(F32)
        for k in range(1, kinds):
            total = total + cols[k] * green_ref[0, 0, k, :, lanes].astype(F32)
        total = total.T
        merged[step, lanes, :] = total
        top[...] = jnp.maximum(top[...], jnp.max(jnp.abs(total).reshape(subs // 8, 8, subs), axis=0))

    @pl.when(step == 3)
    def _():
        most = jnp.maximum(jnp.max(top[...], axis=0, keepdims=True), LEAST)
        power = jnp.ceil(jnp.log2(most * (1.0 / CODE_TOP)))
        power = jnp.maximum(power, -126.0)
        inverse = jnp.exp2(-power)
        slip = (slip_ref[...].astype(F32) * SLIP_UNIT).astype(I32).astype(I16)
        head = jnp.concatenate([onset_ref[...], jnp.broadcast_to(power.astype(I32), (8, subs))], axis=0).astype(I16)
        for g in range(groups):
            for i in range(4):
                part = merged[i, pl.ds(g, share, stride=groups), :] * inverse
                msg_ref[g, i * share : (i + 1) * share, :] = jnp.round(part).astype(I32).astype(I16)
            msg_ref[g, 4 * share : 4 * share + 128, :] = slip
            msg_ref[g, 4 * share + 128 : 4 * share + 144, :] = head


def table_kernel(groups, samples, place_ref, msg_ref, combo_ref, out_ref, slips, shifted, table):
    share = samples // 2 // groups
    hypos = shifted.shape[0]
    subs = msg_ref.shape[2]
    mine = place_ref[0]
    freq = mine + groups * lax.broadcasted_iota(I32, (16, subs), 0)

    def one_source(src, carry):
        lanes = pl.ds(pl.multiple_of(src * subs, subs), subs)
        slip = msg_ref[src, 4 * share : 4 * share + 128, :].astype(I32).astype(F32) * (1.0 / SLIP_UNIT)
        slips[:, lanes] = slip.astype(BF16)
        head = msg_ref[src, 4 * share + 128 : 4 * share + 144, :].astype(I32)
        unit = jnp.exp2(head[8:9].astype(F32))
        jump_c, jump_s = cos_sin((head[0:8] * (16 * groups)) & (samples - 1), samples)
        for h in range(hypos):
            onset = jnp.broadcast_to(head[h : h + 1], (16, subs))
            cosine, sine = cos_sin((onset * freq) & (samples - 1), samples)
            cosine, sine = cosine * unit, sine * unit
            jc = jnp.broadcast_to(jump_c[h : h + 1], (16, subs))
            js = jnp.broadcast_to(jump_s[h : h + 1], (16, subs))
            for a in range(share // 16):
                if a:
                    cosine, sine = cosine * jc - sine * js, sine * jc + cosine * js
                for comp in range(2):
                    r0 = comp * share + a * 16
                    re = msg_ref[src, r0 : r0 + 16, :].astype(I32).astype(F32)
                    im = msg_ref[src, 2 * share + r0 : 2 * share + r0 + 16, :].astype(I32).astype(F32)
                    x0 = comp * 2 * share + a * 16
                    shifted[h, x0 : x0 + 16, lanes] = (cosine * re + sine * im).astype(BF16)
                    shifted[h, x0 + share : x0 + share + 16, lanes] = (cosine * im - sine * re).astype(BF16)
        return carry

    lax.fori_loop(0, groups, one_source, 0)
    pats = slips.shape[0]
    for h in range(hypos):
        rows = lax.dot_general(slips[...], shifted[h], (((1,), (1,)), ((), ())), preferred_element_type=F32)
        table[h * pats : (h + 1) * pats, :] = rows.astype(BF16)
    combo = combo_ref[...]
    chosen = jnp.zeros(out_ref.shape[:1] + (1,), F32)
    count = combo.shape[0]
    spectra = None
    for h in range(hypos):
        ids = lax.broadcasted_iota(I32, (count, pats), 1) + h * pats
        pick = jnp.where(combo == ids, 1.0, 0.0).astype(BF16)
        term = jnp.dot(pick, table[h * pats : (h + 1) * pats, :], preferred_element_type=F32)
        spectra = term if spectra is None else spectra + term
    dests = out_ref.shape[0]
    parts = [spectra[:, i * 128 : (i + 1) * 128].reshape(dests, count // dests, 128) for i in range(spectra.shape[1] // 128)]
    out_ref[...] = jnp.concatenate(parts, axis=1).astype(BF16)


def sum_kernel(in_ref, out_ref):
    total = jnp.sum(in_ref[...].astype(F32), axis=0)
    rows = out_ref.shape[0]
    for i in range(rows):
        for half in range(2):
            out_ref[i, half : half + 1, :] = total[half * rows + i : half * rows + i + 1, :]


def inverse_tables(groups, freqs, samples):
    share = freqs // groups
    k, b, g, a = np.arange(share), np.arange(128), np.arange(groups), np.arange(samples // 128)
    turn = 2.0 * math.pi / samples
    first = turn * (groups * k[:, None] * b[None, :] % samples)
    c, s = np.cos(first), np.sin(first)
    main = np.concatenate([np.concatenate([c, s], 1), np.concatenate([-s, c], 1)], 0) / math.sqrt(freqs)
    second = np.repeat(turn * (g[:, None] * b[None, :] % samples), 2, axis=0)
    twist = np.stack([np.cos(second), np.sin(second)])
    third = turn * (128 * g[:, None] * a[None, :] % samples)
    last = np.stack([np.cos(third), -np.sin(third)])[..., None] * np.ones((1, 1, 1, 128))
    return [t.astype(np.float32) for t in (main, twist, last)]


def inverse_kernel(in_ref, main_ref, twist_ref, last_ref, out_ref):
    groups, comps, width = in_ref.shape
    rows = in_ref[...].reshape(groups * comps, width)
    row = lax.broadcasted_iota(I32, rows.shape, 0)
    lane = lax.broadcasted_iota(I32, rows.shape, 1)
    rows = jnp.where((row < comps) & (lane % (width // 2) == 0), 0.5 * rows, rows)
    v = jnp.dot(rows, main_ref[...], precision=lax.Precision.HIGHEST, preferred_element_type=F32)
    vr, vi = v[:, :128], v[:, 128:]
    c, s = twist_ref[0], twist_ref[1]
    ur, ui = vr * c - vi * s, vr * s + vi * c
    for comp in range(comps):
        total = None
        for g in range(groups):
            r = g * comps + comp
            term = last_ref[0, g] * ur[r : r + 1] + last_ref[1, g] * ui[r : r + 1]
            total = term if total is None else total + term
        for a in range(total.shape[0]):
            out_ref[0, comp : comp + 1, a * 128 : (a + 1) * 128] = total[a : a + 1]


def on_device(green, mechanism, slip, onset, pattern_of_variation, hypo_of_variation):
    _, comps, kinds, subs, freqs = green.shape
    samples = 2 * freqs
    pats, hypos = slip.shape[0], onset.shape[0]
    groups = lax.axis_size(GROUP)
    planes = lax.axis_size(PLANE)
    count = pattern_of_variation.shape[0]
    share = freqs // groups
    lines = 4 * share + pats + 16
    params = pltpu.CompilerParams(vmem_limit_bytes=VMEM)

    msg = pl.pallas_call(
        lambda *refs: merge_kernel(groups, *refs),
        out_shape=jax.ShapeDtypeStruct((groups, lines, subs), I16),
        grid=(2, comps),
        in_specs=[
            pl.BlockSpec((1, 1, kinds, subs, freqs), lambda q, c: (q, c, 0, 0, 0)),
            pl.BlockSpec((kinds, subs), lambda q, c: (0, 0)),
            pl.BlockSpec((pats, subs), lambda q, c: (0, 0)),
            pl.BlockSpec((hypos, subs), lambda q, c: (0, 0)),
        ],
        out_specs=pl.BlockSpec((groups, lines, subs), lambda q, c: (0, 0, 0)),
        scratch_shapes=[
            pltpu.VMEM((kinds, subs, subs), F32),
            pltpu.VMEM((2 * comps, freqs, subs), F32),
            pltpu.VMEM((8, subs), F32),
        ],
        compiler_params=params,
        name="merge",
    )(green, mechanism, slip, onset)

    msg = lax.all_to_all(msg, GROUP, 0, 0, tiled=True)

    combos = hypo_of_variation * pats + pattern_of_variation
    gx, gc = lax.axis_size("x"), lax.axis_size("c")
    combos = combos.reshape(gx, planes, gc).transpose(1, 0, 2).reshape(count, 1)
    place = lax.axis_index(GROUP).astype(I32).reshape(1)
    width = 4 * share
    parts = pl.pallas_call(
        lambda *refs: table_kernel(groups, samples, *refs),
        out_shape=jax.ShapeDtypeStruct((planes, count // planes * (width // 128), 128), BF16),
        in_specs=[
            pl.BlockSpec(memory_space=pltpu.SMEM),
            pl.BlockSpec(memory_space=pltpu.VMEM),
            pl.BlockSpec(memory_space=pltpu.VMEM),
        ],
        out_specs=pl.BlockSpec(memory_space=pltpu.VMEM),
        scratch_shapes=[
            pltpu.VMEM((pats, groups * subs), BF16),
            pltpu.VMEM((hypos, width, groups * subs), BF16),
            pltpu.VMEM((hypos * pats, width), BF16),
        ],
        compiler_params=params,
        name="table",
    )(place, msg, combos)

    parts = lax.all_to_all(parts, PLANE, 0, 0, tiled=True)

    summed = pl.pallas_call(
        sum_kernel,
        out_shape=jax.ShapeDtypeStruct((count // planes, width // 128, 128), F32),
        compiler_params=params,
        name="sum",
    )(parts)

    spectra = lax.all_to_all(summed, GROUP, 0, 0, tiled=True)

    tables = [jnp.asarray(t) for t in inverse_tables(groups, freqs, samples)]
    return pl.pallas_call(
        inverse_kernel,
        out_shape=jax.ShapeDtypeStruct((1, comps, samples), F32),
        compiler_params=params,
        name="inverse",
    )(spectra, *tables)


def solution(mesh):
    blk, sub = mesh.devices.shape
    fine = Mesh(mesh.devices.reshape(4, blk // 4, sub // 4, 2, 2), AXES)
    in_specs = (
        P(None, None, None, AXES, None),
        P(None, AXES),
        P(None, AXES),
        P(None, AXES),
        P(),
        P(),
    )
    out_specs = P(AXES, None, None)
    return jax.shard_map(on_device, mesh=fine, in_specs=in_specs, out_specs=out_specs, check_vma=False)
```

time: 586 us -> 68.9 us (0.12)
  waiting for transfers between devices: 398 us -> 12.3 us
  local copies, waits for them, and re-layouts: 78.6 us -> 4.4 us
  other arithmetic: 41.7 us -> 0.01 us
  blocking collectives: 0 us -> 33.5 us
  starting transfers between devices: 41.1 us -> 10.5 us
  between operations: 13.5 us -> 0.06 us
  matrix products: 11 us -> 0 us
  Pallas kernels: 0 us -> 7.85 us
    unnamed x2 -> x0, waiting for transfers between devices: 260 us -> none
    ppermute x16 -> x0, waiting for transfers between devices: 137 us -> none  [shifted_2(): return lax.ppermute(block, axis, route)]
    gather x16 -> x0, local copies, waits for them, and re-layouts: 66.4 us -> none  [forward_step(): return arrived + jnp.take(table, block_ids(block), axis=0)]
    ppermute x16 -> x0, starting transfers between devices: 41.1 us -> none  [shifted_2(): return lax.ppermute(block, axis, route)]
    all_to_all x0 -> x2, blocking collectives: none -> 33.5 us  [the longest x1 23.5 us: on_device(): parts = lax.all_to_all(parts, PLANE, 0, 0, tiled=True)]
    another operation x2 -> x0, other arithmetic: 19.5 us -> none  [the longest x1 10.5 us: build_table(): shifted = jnp.stack([shifted_re, shifted_im], axis=3).astype(jnp.bfloat16)]
    all_to_all x0 -> x1, waiting for transfers between devices: none -> 12.3 us  [on_device(): msg = lax.all_to_all(msg, GROUP, 0, 0, tiled=True)]
    dot_general x2 -> x0, matrix products: 11 us -> none  [the longest x1 6.69 us: build_table(): jnp.einsum('ps,hsx->hpx', slip, shifted, preferred_element_type=jnp.float32)]
  transfers between devices with their start and end apart: 17 -> 1, of which waited for: 17 -> 1; matrix products, arithmetic and copies ran while one was open for 13% -> 1% of each run, Pallas kernels for 0% -> 0%
where the time goes in v1:
time: 68.9 us; the launch traced here: 68.5 us
  blocking collectives  33.5 us (49%)
  waiting for transfers between devices  12.3 us (18%)
  starting transfers between devices  10.5 us (15%)
  Pallas kernels  7.85 us (11%)
  local copies, waits for them, and re-layouts  4.4 us (6%)
    all_to_all x1, blocking collectives, on_device(): parts = lax.all_to_all(parts, PLANE, 0, 0, tiled=True)  23.5 us
    all_to_all x1, waiting for transfers between devices, on_device(): msg = lax.all_to_all(msg, GROUP, 0, 0, tiled=True)  12.3 us
    all_to_all x1, starting transfers between devices, on_device(): msg = lax.all_to_all(msg, GROUP, 0, 0, tiled=True)  10.5 us
    all_to_all x1, blocking collectives, on_device(): spectra = lax.all_to_all(summed, GROUP, 0, 0, tiled=True)  10.1 us
    pallas_call x1, Pallas kernels, on_device(): pl.pallas_call(lambda *refs: table_kernel(groups, samples, *refs), out_sh...  4.75 us
    unnamed x18, local copies, waits for them, and re-layouts  4.04 us
    pallas_call x1, Pallas kernels, on_device(): pl.pallas_call(lambda *refs: merge_kernel(groups, *refs), out_shape=jax.S...  2.23 us
  transfers between devices with their start and end apart: 1, of which 1 were waited for; matrix products, arithmetic and copies ran while one was open for 1% of the time, Pallas kernels for 0%

profile of v1, /device:TPU:1, one launch (start us, length us, event | category | flops | bytes accessed | tf_op | source)
XLA Modules:
  0.0 68.5 jit_solution(4322325092833558057)
XLA Ops:
  0.0 0.0 copy-start
  0.0 1.9 %copy-done = bf16[2,2,6,128,512]{4,3,2,1,0:T(8,128)(2,1)S(1)} copy-done((bf16[2,2,6,128,512]{4,3,2,1,0:T(8,128)(2,1)S(1)}, bf16[2,2,6,128,512]{4,3,2,1,0:T(8,128)(2,1)}, u32[]{:S(2)}) %copy-start) | copy-done | bytes 3145752
  1.9 0.0 copy-start.3
  1.9 0.8 %copy-done.3 = bf16[128,128]{1,0:T(8,128)(2,1)S(1)} copy-done((bf16[128,128]{1,0:T(8,128)(2,1)S(1)}, bf16[128,128]{1,0:T(8,128)(2,1)}, u32[]{:S(2)}) %copy-start.3) | copy-done | bytes 32792
  2.6 0.0 copy-start.5
  2.7 0.7 copy-done.5
  3.3 0.0 copy-start.6
  3.3 0.7 copy-done.6
  4.0 0.0 copy-start.7
  4.0 0.0 copy-start.8
  4.0 2.2 %merge.1 = s16[8,400,128]{2,1,0:T(8,128)(2,1)} custom-call(bf16[2,2,6,128,512]{4,3,2,1,0:T(8,128)(2,1)S(1)} %copy-done, f32[6,128]{1,0:T(8,128)S(1)} %copy-done.5, bf16[128,128]{1,0:T(8,128)(2,1)S(1)} %copy-done.3, s32[8,128]{1,0:T(8,128)S(1)} %copy-done.6), custom_call_target="tpu_custom_call" | custom-call | tf_op jit(solution)/shard_map/merge/pallas_call | solution.py:178
  6.3 0.0 copy-start.1
  6.3 0.0 copy-start.2
  6.3 0.0 copy-start.4
  6.3 10.5 %all-to-all-start = ((s16[8,400,128]{2,1,0:T(8,128)(2,1)}), s16[8,400,128]{2,1,0:T(8,128)(2,1)S(1)}, u32[]{:S(2)}, u32[]{:S(2)}) async-start(s16[8,400,128]{2,1,0:T(8,128)(2,1)} %merge.1), calls=%async_computation | async-start | bytes 1638400 | tf_op jit(solution)/shard_map/all_to_all | solution.py:198
  16.7 0.0 copy-done.7
  16.7 0.0 copy-done.8
  16.7 0.1 reshape.10
  16.9 0.1 copy.10
  17.0 0.1 reshape.12.refs_2_
  17.1 12.3 %all-to-all-done.refs_1_ = s16[8,400,128]{2,1,0:T(8,128)(2,1)S(1)} async-done(((s16[8,400,128]{2,1,0:T(8,128)(2,1)}), s16[8,400,128]{2,1,0:T(8,128)(2,1)S(1)}, u32[]{:S(2)}, u32[]{:S(2)}) %all-to-all-start) | async-done | bytes 819232 | tf_op jit(solution)/shard_map/all_to_all | solution.py:198
  29.4 4.7 %table.1 = bf16[64,16,128]{2,1,0:T(8,128)(2,1)S(1)} custom-call(s32[1]{0:T(128)} %bitcast.refs_0_, s16[8,400,128]{2,1,0:T(8,128)(2,1)S(1)} %all-to-all-done.refs_1_, s32[512,1]{1,0:T(8,128)S(1)} %reshape.12.refs_2_), custom_call_target="tpu_custom_call" | custom-call | tf_op jit(solution)/shard_map/table/pallas_call | solution.py:205
  34.1 23.5 %all_to_all.15.in_ref = bf16[64,16,128]{2,1,0:T(8,128)(2,1)S(1)} all-to-all(bf16[64,16,128]{2,1,0:T(8,128)(2,1)S(1)} %table.1), channel_id=1, replica_groups=mesh['x'=4,'zh'=4,'y'=8,'zl'=2,'c'=2] {'zh','y','zl'}, dimensions={0} | all-to-all | bytes 524288 | tf_op jit(solution)/shard_map/all_to_all | solution.py:223
  57.6 0.1 sum.1
  57.7 10.1 %all_to_all.16.in_ref = f32[8,2,128]{2,1,0:T(2,128)S(1)} all-to-all(f32[8,2,128]{2,1,0:T(2,128)S(1)} %sum.1), channel_id=1, replica_groups=mesh['x'=4,'zh'=4,'y'=8,'zl'=2,'c'=2] {'x','c'}, dimensions={0} | all-to-all | bytes 16384 | tf_op jit(solution)/shard_map/all_to_all | solution.py:232
  67.7 0.0 copy-done.1
  67.7 0.0 copy-done.2
  67.7 0.0 copy-done.4
  67.7 0.8 %inverse.1 = f32[1,2,1024]{2,1,0:T(2,128)} custom-call(f32[8,2,128]{2,1,0:T(2,128)S(1)} %all_to_all.16.in_ref, f32[128,256]{1,0:T(8,128)S(1)} %copy-done.1, f32[2,16,128]{2,1,0:T(8,128)S(1)} %copy-done.4, f32[2,8,8,128]{3,2,1,0:T(8,128)S(1)} %copy-done.2), custom_call_target="tpu_custom_call" | custom-call | tf_op jit(solution)/shard_map/inverse/pallas_call | solution.py:235
  (1 shorter events, 0.0 us)
Async XLA Ops:
  0.0 1.9 %copy-start = (bf16[2,2,6,128,512]{4,3,2,1,0:T(8,128)(2,1)S(1)}, bf16[2,2,6,128,512]{4,3,2,1,0:T(8,128)(2,1)}, u32[]{:S(2)}) copy-start(bf16[2,2,6,128,512]{4,3,2,1,0:T(8,128)(2,1)} %refs_0_.1) | copy-start | bytes 9437188
  1.9 0.8 %copy-start.3 = (bf16[128,128]{1,0:T(8,128)(2,1)S(1)}, bf16[128,128]{1,0:T(8,128)(2,1)}, u32[]{:S(2)}) copy-start(bf16[128,128]{1,0:T(8,128)(2,1)} %refs_2_.1) | copy-start | bytes 98308
  2.6 0.7 %copy-start.5 = (f32[6,128]{1,0:T(8,128)S(1)}, f32[6,128]{1,0:T(8,128)}, u32[]{:S(2)}) copy-start(f32[6,128]{1,0:T(8,128)} %refs_1_.1) | copy-start | bytes 9220
  3.3 0.7 %copy-start.6 = (s32[8,128]{1,0:T(8,128)S(1)}, s32[8,128]{1,0:T(8,128)}, u32[]{:S(2)}) copy-start(s32[8,128]{1,0:T(8,128)} %refs_3_.1) | copy-start | bytes 12292
  4.0 12.7 %copy-start.7 = (s32[512]{0:T(512)S(1)}, s32[512]{0:T(512)}, u32[]{:S(2)}) copy-start(s32[512]{0:T(512)} %param.13) | copy-start | bytes 6148
  4.0 12.7 %copy-start.8 = (s32[512]{0:T(512)S(1)}, s32[512]{0:T(512)}, u32[]{:S(2)}) copy-start(s32[512]{0:T(512)} %param.14) | copy-start | bytes 6148
  6.3 61.5 %copy-start.1 = (f32[128,256]{1,0:T(8,128)S(1)}, f32[128,256]{1,0:T(8,128)}, u32[]{:S(2)}) copy-start(f32[128,256]{1,0:T(8,128)} %constant.20.clone.main_ref) | copy-start | bytes 393220
  6.3 61.5 %copy-start.2 = (f32[2,8,8,128]{3,2,1,0:T(8,128)S(1)}, f32[2,8,8,128]{3,2,1,0:T(8,128)}, u32[]{:S(2)}) copy-start(f32[2,8,8,128]{3,2,1,0:T(8,128)} %constant.22.clone.last_ref) | copy-start | bytes 196612
  6.3 61.5 %copy-start.4 = (f32[2,16,128]{2,1,0:T(8,128)S(1)}, f32[2,16,128]{2,1,0:T(8,128)}, u32[]{:S(2)}) copy-start(f32[2,16,128]{2,1,0:T(8,128)} %constant.21.clone.twist_ref) | copy-start | bytes 49156
  6.3 23.1 %all-to-all-start = ((s16[8,400,128]{2,1,0:T(8,128)(2,1)}), s16[8,400,128]{2,1,0:T(8,128)(2,1)S(1)}, u32[]{:S(2)}, u32[]{:S(2)}) async-start(s16[8,400,128]{2,1,0:T(8,128)(2,1)} %merge.1), calls=%async_computation | async-start | bytes 1638400 | tf_op jit(solution)/shard_map/all_to_all | solution.py:198

commit v2 on v1

v2 whole, which is shorter than its diff:
```python
import math

import jax
import jax.numpy as jnp
import numpy as np
from jax import lax
from jax.experimental import pallas as pl
from jax.experimental.pallas import tpu as pltpu
from jax.sharding import Mesh
from jax.sharding import PartitionSpec as P

AXES = ("x", "zh", "y", "zl", "c")
GROUP = ("x", "c")
PLANE = ("zh", "y", "zl")
CODE_TOP = 32000.0
SLIP_UNIT = 2048.0
LEAST = 4e-34
F32, BF16, I32, I16 = jnp.float32, jnp.bfloat16, jnp.int32, jnp.int16
VMEM = 48 * 1024 * 1024
MERGE_VMEM = 63 * 1024 * 1024


def cos_sin(steps, samples):
    eighth = samples // 8
    quadrant = (steps + eighth) >> int(math.log2(samples // 4))
    rest = steps - quadrant * (samples // 4)
    t = rest.astype(F32) * (2.0 * math.pi / samples)
    t2 = t * t
    sine = t + t * t2 * (-1.0 / 6 + t2 * (1.0 / 120 + t2 * (-1.0 / 5040 + t2 * (1.0 / 362880))))
    cosine = 1.0 + t2 * (-0.5 + t2 * (1.0 / 24 + t2 * (-1.0 / 720 + t2 * (1.0 / 40320))))
    odd = (quadrant & 1) == 1
    c = jnp.where(odd, sine, cosine)
    s = jnp.where(odd, cosine, sine)
    c = jnp.where(((quadrant + 1) & 2) == 2, -c, c)
    s = jnp.where((quadrant & 2) == 2, -s, s)
    return c, s


def merge_kernel(groups, green_ref, mech_ref, slip_ref, onset_ref, out_ref, green, mech, slip, onset, merged, msg, sems, out_sems):
    _, comps, kinds, subs, freqs = green_ref.shape
    share = freqs // groups
    end = 2 * comps * share
    blocks = [(c, q) for c in range(comps) for q in range(2)]
    copies = [pltpu.make_async_copy(mech_ref, mech, sems.at[0])]
    for i, (c, q) in enumerate(blocks):
        copies.append(pltpu.make_async_copy(green_ref.at[q, c], green.at[i], sems.at[1 + i]))
    copies.append(pltpu.make_async_copy(slip_ref, slip, sems.at[1 + 2 * comps]))
    copies.append(pltpu.make_async_copy(onset_ref, onset, sems.at[2 + 2 * comps]))
    for copy in copies:
        copy.start()
    copies[0].wait()
    cols = [jnp.broadcast_to(mech[k : k + 1, :], (subs, subs)).T for k in range(kinds)]
    powers, sends = [], []
    for i in range(2 * comps):
        copies[1 + i].wait()
        top = jnp.zeros((8, subs), F32)
        for tile in range(freqs // subs):
            piece = slice(tile * subs, (tile + 1) * subs)
            total = cols[0] * green[i, 0, :, piece].astype(F32)
            for k in range(1, kinds):
                total = total + cols[k] * green[i, k, :, piece].astype(F32)
            total = total.T
            merged[i, piece, :] = total
            top = jnp.maximum(top, jnp.max(jnp.abs(total).reshape(subs // 8, 8, subs), axis=0))
        most = jnp.maximum(jnp.max(top, axis=0, keepdims=True), LEAST)
        power = jnp.maximum(jnp.ceil(jnp.log2(most * (1.0 / CODE_TOP))), -126.0)
        powers.append(power.astype(I32))
        inverse = jnp.exp2(-power)
        lines = slice(i * share, (i + 1) * share)
        for g in range(groups):
            part = merged[i, pl.ds(g, share, stride=groups), :] * inverse
            msg[g, lines, :] = jnp.round(part).astype(I32).astype(I16)
        sends.append(pltpu.make_async_copy(msg.at[:, lines], out_ref.at[:, lines], out_sems.at[i]))
        sends[-1].start()
        if i == 0:
            copies[-2].wait()
            codes = (slip[...].astype(F32) * SLIP_UNIT).astype(I32).astype(I16)
            for g in range(groups):
                msg[g, end + 16 :, :] = codes
            tail = slice(end + 16, msg.shape[1])
            sends.append(pltpu.make_async_copy(msg.at[:, tail], out_ref.at[:, tail], out_sems.at[2 * comps]))
            sends[-1].start()
    copies[-1].wait()
    head = jnp.concatenate([jnp.broadcast_to(p, (8 // len(powers), subs)) for p in powers] + [onset[...]], axis=0).astype(I16)
    for g in range(groups):
        msg[g, end : end + 16, :] = head
    sends.append(pltpu.make_async_copy(msg.at[:, end : end + 16], out_ref.at[:, end : end + 16], out_sems.at[2 * comps + 1]))
    sends[-1].start()
    for send in sends:
        send.wait()


def pick_kernel(combo_ref, pick_ref):
    count, entries = pick_ref.shape
    for first in range(0, entries, 128):
        ids = lax.broadcasted_iota(I32, (count, 128), 1) + first
        pick_ref[:, first : first + 128] = jnp.where(combo_ref[...] == ids, 1.0, 0.0).astype(BF16)


def table_kernel(groups, samples, place_ref, msg_ref, pick_ref, out_ref, slips, values, shifted, turns):
    hypos, rows, _ = shifted.shape
    subs = values.shape[2]
    pats = slips.shape[0]
    share = rows // 4
    mine = place_ref[0]
    freq = mine + groups * lax.broadcasted_iota(I32, (8, subs), 0)

    for src in range(groups):
        lanes = slice(src * subs, (src + 1) * subs)
        slip = msg_ref[src, rows + 16 :, :].astype(I32).astype(F32) * (1.0 / SLIP_UNIT)
        slips[:, lanes] = slip.astype(BF16)
        head = msg_ref[src, rows : rows + 16, :].astype(I32)
        for i in range(4):
            lines = slice(i * share, (i + 1) * share)
            unit = jnp.exp2(head[2 * i : 2 * i + 1].astype(F32))
            values[src, lines, :] = msg_ref[src, lines, :].astype(I32).astype(F32) * unit
        near_c, near_s = cos_sin((head[8:16] * (8 * groups)) & (samples - 1), samples)
        turns[src, 0] = near_c
        turns[src, 1] = near_s
        turns[src, 2] = near_c * near_c - near_s * near_s
        turns[src, 3] = 2.0 * near_c * near_s

    spectra = None
    for h in range(hypos):
        for src in range(groups):
            lanes = slice(src * subs, (src + 1) * subs)
            row = rows + 8 + h
            onset = jnp.broadcast_to(msg_ref[src, rows : rows + 16, :].astype(I32)[8 + h : 9 + h], (8, subs))
            c0, s0 = cos_sin((onset * freq) & (samples - 1), samples)
            nc, ns = turns[src, 0, h : h + 1, :], turns[src, 1, h : h + 1, :]
            c = jnp.concatenate([c0, c0 * nc - s0 * ns], axis=0)
            s = jnp.concatenate([s0, s0 * nc + c0 * ns], axis=0)
            jc = jnp.broadcast_to(turns[src, 2, h : h + 1, :], (16, subs))
            js = jnp.broadcast_to(turns[src, 3, h : h + 1, :], (16, subs))
            for a in range(share // 16):
                if a:
                    c, s = c * jc - s * js, s * jc + c * js
                for comp in range(2):
                    r0 = comp * 2 * share + a * 16
                    re = values[src, r0 : r0 + 16, :]
                    im = values[src, r0 + share : r0 + share + 16, :]
                    shifted[h, r0 : r0 + 16, lanes] = (c * re + s * im).astype(BF16)
                    shifted[h, r0 + share : r0 + share + 16, lanes] = (c * im - s * re).astype(BF16)
        sums = lax.dot_general(slips[...], shifted[h], (((1,), (1,)), ((), ())), preferred_element_type=F32)
        sums = sums.astype(BF16)
        if h % 2 == 0:
            held = sums
        else:
            both = jnp.concatenate([held, sums], axis=0)
            chosen = jnp.dot(pick_ref[:, (h - 1) * pats : (h + 1) * pats], both, preferred_element_type=F32)
            spectra = chosen if spectra is None else spectra + chosen
    dests = out_ref.shape[0]
    parts = [spectra[:, i : i + 128].reshape(dests, -1, 128) for i in range(0, rows, 128)]
    out_ref[...] = jnp.concatenate(parts, axis=1).astype(BF16)


def sum_kernel(in_ref, out_ref):
    total = jnp.sum(in_ref[...].astype(F32), axis=0)
    rows = out_ref.shape[0]
    for i in range(rows):
        for half in range(2):
            out_ref[i, half : half + 1, :] = total[half * rows + i : half * rows + i + 1, :]


def inverse_tables(groups, freqs, samples):
    share = freqs // groups
    k, b, g, a = np.arange(share), np.arange(128), np.arange(groups), np.arange(samples // 128)
    turn = 2.0 * math.pi / samples
    first = turn * (groups * k[:, None] * b[None, :] % samples)
    c, s = np.cos(first), np.sin(first)
    main = np.concatenate([np.concatenate([c, s], 1), np.concatenate([-s, c], 1)]) / math.sqrt(freqs)
    second = np.tile(turn * (g[:, None] * b[None, :] % samples), (2, 1))
    twist = np.stack([np.cos(second), np.sin(second)])
    third = turn * (128 * g[:, None] * a[None, :] % samples)
    last = np.stack([np.cos(third), -np.sin(third)])[..., None] * np.ones((1, 1, 1, 128))
    return [t.astype(np.float32) for t in (main, twist, last)]


def inverse_kernel(in_ref, main_ref, twist_ref, last_ref, out_ref):
    groups, comps, width = in_ref.shape
    rows = jnp.concatenate([in_ref[:, comp, :] for comp in range(comps)], axis=0)
    row = lax.broadcasted_iota(I32, rows.shape, 0)
    lane = lax.broadcasted_iota(I32, rows.shape, 1)
    zero = (row % groups == 0) & (lane % (width // 2) == 0)
    rows = jnp.where(zero, 0.5 * rows, rows)
    v = jnp.dot(rows, main_ref[...], precision=lax.Precision.HIGHEST, preferred_element_type=F32)
    vr, vi = v[:, :128], v[:, 128:]
    c, s = twist_ref[0], twist_ref[1]
    ur, ui = vr * c - vi * s, vr * s + vi * c
    for comp in range(comps):
        total = None
        for g in range(groups):
            r = comp * groups + g
            term = last_ref[0, g] * ur[r : r + 1] + last_ref[1, g] * ui[r : r + 1]
            total = term if total is None else total + term
        for a in range(total.shape[0]):
            out_ref[0, comp : comp + 1, a * 128 : (a + 1) * 128] = total[a : a + 1]


def merge_call(groups, green, mechanism, slip, onset):
    _, comps, kinds, subs, freqs = green.shape
    pats, hypos = slip.shape[0], onset.shape[0]
    lines = 2 * comps * freqs // groups + 16 + pats
    return pl.pallas_call(
        lambda *refs: merge_kernel(groups, *refs),
        out_shape=jax.ShapeDtypeStruct((groups, lines, subs), I16),
        in_specs=[pl.BlockSpec(memory_space=pltpu.HBM)] * 4,
        out_specs=pl.BlockSpec(memory_space=pltpu.HBM),
        scratch_shapes=[
            pltpu.VMEM((2 * comps, kinds, subs, freqs), BF16),
            pltpu.VMEM((kinds, subs), F32),
            pltpu.VMEM((pats, subs), BF16),
            pltpu.VMEM((hypos, subs), I32),
            pltpu.VMEM((2 * comps, freqs, subs), F32),
            pltpu.VMEM((groups, lines, subs), I16),
            pltpu.SemaphoreType.DMA((2 * comps + 3,)),
            pltpu.SemaphoreType.DMA((2 * comps + 2,)),
        ],
        compiler_params=pltpu.CompilerParams(vmem_limit_bytes=MERGE_VMEM),
        name="merge",
    )(green, mechanism, slip, onset)


def table_call(groups, samples, planes, hypos, pats, place, msg, pick):
    subs = msg.shape[2]
    rows = msg.shape[1] - 16 - pats
    in_vmem = pl.BlockSpec(memory_space=pltpu.VMEM)
    return pl.pallas_call(
        lambda *refs: table_kernel(groups, samples, *refs),
        out_shape=jax.ShapeDtypeStruct((planes, pick.shape[0] // planes * (rows // 128), 128), BF16),
        in_specs=[pl.BlockSpec(memory_space=pltpu.SMEM), in_vmem, in_vmem],
        out_specs=in_vmem,
        scratch_shapes=[
            pltpu.VMEM((pats, groups * subs), BF16),
            pltpu.VMEM((groups, rows, subs), F32),
            pltpu.VMEM((hypos, rows, groups * subs), BF16),
            pltpu.VMEM((groups, 4, hypos, subs), F32),
        ],
        compiler_params=pltpu.CompilerParams(vmem_limit_bytes=VMEM),
        name="table",
    )(place, msg, pick)


def on_device(green, mechanism, slip, onset, pattern_of_variation, hypo_of_variation):
    _, comps, kinds, subs, freqs = green.shape
    samples = 2 * freqs
    pats, hypos = slip.shape[0], onset.shape[0]
    groups = lax.axis_size(GROUP)
    planes = lax.axis_size(PLANE)
    count = pattern_of_variation.shape[0]
    rows = 2 * comps * freqs // groups
    params = pltpu.CompilerParams(vmem_limit_bytes=VMEM)
    in_vmem = pl.BlockSpec(memory_space=pltpu.VMEM)

    msg = merge_call(groups, green, mechanism, slip, onset)
    msg = lax.all_to_all(msg, GROUP, 0, 0, tiled=True)

    combos = hypo_of_variation * pats + pattern_of_variation
    gx, gc = lax.axis_size("x"), lax.axis_size("c")
    combos = combos.reshape(gx, planes, gc).transpose(1, 0, 2).reshape(count, 1)
    pick = pl.pallas_call(
        pick_kernel,
        out_shape=jax.ShapeDtypeStruct((count, hypos * pats), BF16),
        in_specs=[in_vmem],
        out_specs=in_vmem,
        compiler_params=params,
        name="pick",
    )(combos)
    place = lax.axis_index(GROUP).astype(I32).reshape(1)
    parts = table_call(groups, samples, planes, hypos, pats, place, msg, pick)

    parts = lax.all_to_all(parts, PLANE, 0, 0, tiled=True)

    summed = pl.pallas_call(
        sum_kernel,
        out_shape=jax.ShapeDtypeStruct((count // planes, rows // 128, 128), F32),
        compiler_params=params,
        name="sum",
    )(parts)

    spectra = lax.all_to_all(summed, GROUP, 0, 0, tiled=True)

    tables = [jnp.asarray(t) for t in inverse_tables(groups, freqs, samples)]
    return pl.pallas_call(
        inverse_kernel,
        out_shape=jax.ShapeDtypeStruct((1, comps, samples), F32),
        compiler_params=params,
        name="inverse",
    )(spectra, *tables)


def solution(mesh):
    blk, sub = mesh.devices.shape
    fine = Mesh(mesh.devices.reshape(4, blk // 4, sub // 4, 2, 2), AXES)
    in_specs = (
        P(None, None, None, AXES, None),
        P(None, AXES),
        P(None, AXES),
        P(None, AXES),
        P(),
        P(),
    )
    out_specs = P(AXES, None, None)
    return jax.shard_map(on_device, mesh=fine, in_specs=in_specs, out_specs=out_specs, check_vma=False)
```

time: 68.9 us -> 64.8 us (0.940)
  local copies, waits for them, and re-layouts: 4.4 us -> 0.39 us
  waiting for transfers between devices: 12.3 us -> 11.6 us
    unnamed x18 -> x10, local copies, waits for them, and re-layouts: 4.04 us -> 0.03 us
    pallas_call x2 -> x3, Pallas kernels: 6.98 us -> 7.54 us  [the longest x1 3.52 us: table_call(): pl.pallas_call(lambda *refs: table_kernel(groups, samples, *refs), out_sh...]
  transfers between devices with their start and end apart: 1 -> 1, of which waited for: 1 -> 1; matrix products, arithmetic and copies ran while one was open for 1% -> 1% of each run, Pallas kernels for 0% -> 1%
where the time goes in v2:
time: 64.8 us; the launch traced here: 64.5 us
  blocking collectives  33.5 us (52%)
  waiting for transfers between devices  11.6 us (18%)
  starting transfers between devices  10.5 us (16%)
  Pallas kernels  8.42 us (13%)
    all_to_all x1, blocking collectives, on_device(): parts = lax.all_to_all(parts, PLANE, 0, 0, tiled=True)  23.5 us
    all_to_all x1, waiting for transfers between devices, on_device(): msg = lax.all_to_all(msg, GROUP, 0, 0, tiled=True)  11.6 us
    all_to_all x1, starting transfers between devices, on_device(): msg = lax.all_to_all(msg, GROUP, 0, 0, tiled=True)  10.5 us
    all_to_all x1, blocking collectives, on_device(): spectra = lax.all_to_all(summed, GROUP, 0, 0, tiled=True)  10.1 us
    pallas_call x1, Pallas kernels, table_call(): pl.pallas_call(lambda *refs: table_kernel(groups, samples, *refs), out_sh...  3.52 us
    pallas_call x1, Pallas kernels, merge_call(): pl.pallas_call(lambda *refs: merge_kernel(groups, *refs), out_shape=jax.S...  3.41 us
  transfers between devices with their start and end apart: 1, of which 1 were waited for; matrix products, arithmetic and copies ran while one was open for 1% of the time, Pallas kernels for 1%

profile of v2, /device:TPU:1, one launch (start us, length us, event | category | flops | bytes accessed | tf_op | source)
XLA Modules:
  0.0 64.5 jit_solution(12599144046950750254)
XLA Ops:
  0.0 0.0 copy-start.3
  0.0 0.0 copy-start.4
  0.0 3.4 %merge.1 = s16[8,400,128]{2,1,0:T(8,128)(2,1)} custom-call(bf16[2,2,6,128,512]{4,3,2,1,0:T(8,128)(2,1)} %refs_0_.1, f32[6,128]{1,0:T(8,128)} %refs_1_.1, bf16[128,128]{1,0:T(8,128)(2,1)} %refs_2_.1, s32[8,128]{1,0:T(8,128)} %refs_3_.1), custom_call_target="tpu_custom_call" | custom-call | tf_op jit(solution)/shard_map/merge/pallas_call | solution.py:204
  3.4 0.0 copy-start
  3.4 0.0 copy-start.1
  3.5 0.0 copy-start.2
  3.5 10.5 %all-to-all-start = ((s16[8,400,128]{2,1,0:T(8,128)(2,1)}), s16[8,400,128]{2,1,0:T(8,128)(2,1)S(1)}, u32[]{:S(2)}, u32[]{:S(2)}) async-start(s16[8,400,128]{2,1,0:T(8,128)(2,1)} %merge.1), calls=%async_computation | async-start | bytes 1638400 | tf_op jit(solution)/shard_map/all_to_all | solution.py:256
  13.9 0.0 copy-done.3
  13.9 0.0 copy-done.4
  14.0 0.1 reshape.10
  14.1 0.1 copy.10
  14.2 0.1 reshape.12.combo_ref
  14.3 0.6 pick.1.refs_2_
  14.9 11.6 %all-to-all-done.refs_1_ = s16[8,400,128]{2,1,0:T(8,128)(2,1)S(1)} async-done(((s16[8,400,128]{2,1,0:T(8,128)(2,1)}), s16[8,400,128]{2,1,0:T(8,128)(2,1)S(1)}, u32[]{:S(2)}, u32[]{:S(2)}) %all-to-all-start) | async-done | bytes 819232 | tf_op jit(solution)/shard_map/all_to_all | solution.py:256
  26.6 3.5 %table.1 = bf16[64,16,128]{2,1,0:T(8,128)(2,1)S(1)} custom-call(s32[1]{0:T(128)} %bitcast.refs_0_, s16[8,400,128]{2,1,0:T(8,128)(2,1)S(1)} %all-to-all-done.refs_1_, bf16[512,1024]{1,0:T(8,128)(2,1)S(1)} %pick.1.refs_2_), custom_call_target="tpu_custom_call" | custom-call | tf_op jit(solution)/shard_map/table/pallas_call | solution.py:228
  30.1 23.5 %all_to_all.15.in_ref = bf16[64,16,128]{2,1,0:T(8,128)(2,1)S(1)} all-to-all(bf16[64,16,128]{2,1,0:T(8,128)(2,1)S(1)} %table.1), channel_id=1, replica_groups=mesh['x'=4,'zh'=4,'y'=8,'zl'=2,'c'=2] {'zh','y','zl'}, dimensions={0} | all-to-all | bytes 524288 | tf_op jit(solution)/shard_map/all_to_all | solution.py:272
  53.6 0.1 sum.1
  53.7 10.1 %all_to_all.16.in_ref = f32[8,2,128]{2,1,0:T(2,128)S(1)} all-to-all(f32[8,2,128]{2,1,0:T(2,128)S(1)} %sum.1), channel_id=1, replica_groups=mesh['x'=4,'zh'=4,'y'=8,'zl'=2,'c'=2] {'x','c'}, dimensions={0} | all-to-all | bytes 16384 | tf_op jit(solution)/shard_map/all_to_all | solution.py:281
  63.7 0.0 copy-done
  63.7 0.0 copy-done.1
  63.7 0.0 copy-done.2
  63.7 0.8 %inverse.1 = f32[1,2,1024]{2,1,0:T(2,128)} custom-call(f32[8,2,128]{2,1,0:T(2,128)S(1)} %all_to_all.16.in_ref, f32[128,256]{1,0:T(8,128)S(1)} %copy-done, f32[2,16,128]{2,1,0:T(8,128)S(1)} %copy-done.2, f32[2,8,8,128]{3,2,1,0:T(8,128)S(1)} %copy-done.1), custom_call_target="tpu_custom_call" | custom-call | tf_op jit(solution)/shard_map/inverse/pallas_call | solution.py:284
  (1 shorter events, 0.0 us)
Async XLA Ops:
  0.0 13.9 %copy-start.3 = (s32[512]{0:T(512)S(1)}, s32[512]{0:T(512)}, u32[]{:S(2)}) copy-start(s32[512]{0:T(512)} %param.13) | copy-start | bytes 6148
  0.0 13.9 %copy-start.4 = (s32[512]{0:T(512)S(1)}, s32[512]{0:T(512)}, u32[]{:S(2)}) copy-start(s32[512]{0:T(512)} %param.14) | copy-start | bytes 6148
  3.4 60.3 %copy-start = (f32[128,256]{1,0:T(8,128)S(1)}, f32[128,256]{1,0:T(8,128)}, u32[]{:S(2)}) copy-start(f32[128,256]{1,0:T(8,128)} %constant.20.clone.main_ref) | copy-start | bytes 393220
  3.4 60.3 %copy-start.1 = (f32[2,8,8,128]{3,2,1,0:T(8,128)S(1)}, f32[2,8,8,128]{3,2,1,0:T(8,128)}, u32[]{:S(2)}) copy-start(f32[2,8,8,128]{3,2,1,0:T(8,128)} %constant.22.clone.last_ref) | copy-start | bytes 196612
  3.5 60.3 %copy-start.2 = (f32[2,16,128]{2,1,0:T(8,128)S(1)}, f32[2,16,128]{2,1,0:T(8,128)}, u32[]{:S(2)}) copy-start(f32[2,16,128]{2,1,0:T(8,128)} %constant.21.clone.twist_ref) | copy-start | bytes 49156
  3.5 23.1 %all-to-all-start = ((s16[8,400,128]{2,1,0:T(8,128)(2,1)}), s16[8,400,128]{2,1,0:T(8,128)(2,1)S(1)}, u32[]{:S(2)}, u32[]{:S(2)}) async-start(s16[8,400,128]{2,1,0:T(8,128)(2,1)} %merge.1), calls=%async_computation | async-start | bytes 1638400 | tf_op jit(solution)/shard_map/all_to_all | solution.py:256

commit v3 on v2

--- a/solution.py
+++ b/solution.py
@@ -2,6 +2,7 @@
 
 import jax
 import jax.numpy as jnp
+import ml_dtypes
 import numpy as np
 from jax import lax
 from jax.experimental import pallas as pl
@@ -97,8 +98,8 @@
         pick_ref[:, first : first + 128] = jnp.where(combo_ref[...] == ids, 1.0, 0.0).astype(BF16)
 
 
-def table_kernel(groups, samples, place_ref, msg_ref, pick_ref, out_ref, slips, values, shifted, turns):
-    hypos, rows, _ = shifted.shape
+def table_kernel(groups, samples, place_ref, msg_ref, pick_ref, out_ref, slips, values, shifted, turns, table):
+    hypos, _, rows = shifted.shape
     subs = values.shape[2]
     pats = slips.shape[0]
     share = rows // 4
@@ -124,7 +125,6 @@
     for h in range(hypos):
         for src in range(groups):
             lanes = slice(src * subs, (src + 1) * subs)
-            row = rows + 8 + h
             onset = jnp.broadcast_to(msg_ref[src, rows : rows + 16, :].astype(I32)[8 + h : 9 + h], (8, subs))
             c0, s0 = cos_sin((onset * freq) & (samples - 1), samples)
             nc, ns = turns[src, 0, h : h + 1, :], turns[src, 1, h : h + 1, :]
@@ -132,6 +132,7 @@
             s = jnp.concatenate([s0, s0 * nc + c0 * ns], axis=0)
             jc = jnp.broadcast_to(turns[src, 2, h : h + 1, :], (16, subs))
             js = jnp.broadcast_to(turns[src, 3, h : h + 1, :], (16, subs))
+            real, imag = [[], []], [[], []]
             for a in range(share // 16):
                 if a:
                     c, s = c * jc - s * js, s * jc + c * js
@@ -139,16 +140,15 @@
                     r0 = comp * 2 * share + a * 16
                     re = values[src, r0 : r0 + 16, :]
                     im = values[src, r0 + share : r0 + share + 16, :]
-                    shifted[h, r0 : r0 + 16, lanes] = (c * re + s * im).astype(BF16)
-                    shifted[h, r0 + share : r0 + share + 16, lanes] = (c * im - s * re).astype(BF16)
-        sums = lax.dot_general(slips[...], shifted[h], (((1,), (1,)), ((), ())), preferred_element_type=F32)
+                    real[comp].append((c * re + s * im).astype(BF16))
+                    imag[comp].append((c * im - s * re).astype(BF16))
+            for comp in range(2):
+                block = jnp.concatenate(real[comp] + imag[comp], axis=0).T
+                shifted[h, lanes, comp * 2 * share : (comp + 1) * 2 * share] = block.astype(BF16)
+        sums = jnp.dot(slips[...], shifted[h], preferred_element_type=F32)
         sums = sums.astype(BF16)
-        if h % 2 == 0:
-            held = sums
-        else:
-            both = jnp.concatenate([held, sums], axis=0)
-            chosen = jnp.dot(pick_ref[:, (h - 1) * pats : (h + 1) * pats], both, preferred_element_type=F32)
-            spectra = chosen if spectra is None else spectra + chosen
+        table[h * pats : (h + 1) * pats, :] = sums
+    spectra = jnp.dot(pick_ref[...], table[...], preferred_element_type=F32)
     dests = out_ref.shape[0]
     parts = [spectra[:, i : i + 128].reshape(dests, -1, 128) for i in range(0, rows, 128)]
     out_ref[...] = jnp.concatenate(parts, axis=1).astype(BF16)
@@ -173,7 +173,11 @@
     twist = np.stack([np.cos(second), np.sin(second)])
     third = turn * (128 * g[:, None] * a[None, :] % samples)
     last = np.stack([np.cos(third), -np.sin(third)])[..., None] * np.ones((1, 1, 1, 128))
-    return [t.astype(np.float32) for t in (main, twist, last)]
+    main = main.astype(np.float32)
+    high = main.astype(ml_dtypes.bfloat16)
+    low = (main - high.astype(np.float32)).astype(ml_dtypes.bfloat16)
+    main = np.concatenate([high, low, high])
+    return [main, twist.astype(np.float32), last.astype(np.float32)]
 
 
 def inverse_kernel(in_ref, main_ref, twist_ref, last_ref, out_ref):
@@ -183,7 +187,9 @@
     lane = lax.broadcasted_iota(I32, rows.shape, 1)
     zero = (row % groups == 0) & (lane % (width // 2) == 0)
     rows = jnp.where(zero, 0.5 * rows, rows)
-    v = jnp.dot(rows, main_ref[...], precision=lax.Precision.HIGHEST, preferred_element_type=F32)
+    high = rows.astype(BF16)
+    low = (rows - high.astype(F32)).astype(BF16)
+    v = jnp.dot(jnp.concatenate([high, high, low], axis=1), main_ref[...], preferred_element_type=F32)
     vr, vi = v[:, :128], v[:, 128:]
     c, s = twist_ref[0], twist_ref[1]
     ur, ui = vr * c - vi * s, vr * s + vi * c
@@ -233,8 +239,9 @@
         scratch_shapes=[
             pltpu.VMEM((pats, groups * subs), BF16),
             pltpu.VMEM((groups, rows, subs), F32),
-            pltpu.VMEM((hypos, rows, groups * subs), BF16),
+            pltpu.VMEM((hypos, groups * subs, rows), BF16),
             pltpu.VMEM((groups, 4, hypos, subs), F32),
+            pltpu.VMEM((hypos * pats, rows), BF16),
         ],
         compiler_params=pltpu.CompilerParams(vmem_limit_bytes=VMEM),
         name="table",

time: 64.8 us -> 64.5 us (level)
  no operation moved by 1% of the time
where the time goes in v3:
time: 64.5 us; the launch traced here: 64.3 us
  blocking collectives  33.5 us (52%)
  waiting for transfers between devices  11.6 us (18%)
  starting transfers between devices  10.5 us (16%)
  Pallas kernels  8.16 us (13%)
    all_to_all x1, blocking collectives, on_device(): parts = lax.all_to_all(parts, PLANE, 0, 0, tiled=True)  23.5 us
    all_to_all x1, waiting for transfers between devices, on_device(): msg = lax.all_to_all(msg, GROUP, 0, 0, tiled=True)  11.6 us
    all_to_all x1, starting transfers between devices, on_device(): msg = lax.all_to_all(msg, GROUP, 0, 0, tiled=True)  10.5 us
    all_to_all x1, blocking collectives, on_device(): spectra = lax.all_to_all(summed, GROUP, 0, 0, tiled=True)  10.1 us
    pallas_call x1, Pallas kernels, merge_call(): pl.pallas_call(lambda *refs: merge_kernel(groups, *refs), out_shape=jax.S...  3.41 us
    pallas_call x1, Pallas kernels, table_call(): pl.pallas_call(lambda *refs: table_kernel(groups, samples, *refs), out_sh...  3.29 us
  transfers between devices with their start and end apart: 1, of which 1 were waited for; matrix products, arithmetic and copies ran while one was open for 1% of the time, Pallas kernels for 1%

profile of v3, /device:TPU:1, one launch (start us, length us, event | category | flops | bytes accessed | tf_op | source)
XLA Modules:
  0.0 64.3 jit_solution(16457390837263047601)
XLA Ops:
  0.0 0.0 copy-start.3
  0.0 0.0 copy-start.4
  0.0 3.4 %merge.1 = s16[8,400,128]{2,1,0:T(8,128)(2,1)} custom-call(bf16[2,2,6,128,512]{4,3,2,1,0:T(8,128)(2,1)} %refs_0_.1, f32[6,128]{1,0:T(8,128)} %refs_1_.1, bf16[128,128]{1,0:T(8,128)(2,1)} %refs_2_.1, s32[8,128]{1,0:T(8,128)} %refs_3_.1), custom_call_target="tpu_custom_call" | custom-call | tf_op jit(solution)/shard_map/merge/pallas_call | solution.py:210
  3.4 0.0 copy-start
  3.4 0.0 copy-start.1
  3.5 0.0 copy-start.2
  3.5 10.5 %all-to-all-start = ((s16[8,400,128]{2,1,0:T(8,128)(2,1)}), s16[8,400,128]{2,1,0:T(8,128)(2,1)S(1)}, u32[]{:S(2)}, u32[]{:S(2)}) async-start(s16[8,400,128]{2,1,0:T(8,128)(2,1)} %merge.1), calls=%async_computation | async-start | bytes 1638400 | tf_op jit(solution)/shard_map/all_to_all | solution.py:263
  13.9 0.0 copy-done.3
  13.9 0.0 copy-done.4
  14.0 0.1 reshape.10
  14.1 0.1 copy.10
  14.2 0.1 reshape.12.combo_ref
  14.3 0.6 pick.1.refs_2_
  14.9 11.6 %all-to-all-done.refs_1_ = s16[8,400,128]{2,1,0:T(8,128)(2,1)S(1)} async-done(((s16[8,400,128]{2,1,0:T(8,128)(2,1)}), s16[8,400,128]{2,1,0:T(8,128)(2,1)S(1)}, u32[]{:S(2)}, u32[]{:S(2)}) %all-to-all-start) | async-done | bytes 819232 | tf_op jit(solution)/shard_map/all_to_all | solution.py:263
  26.6 3.3 %table.1 = bf16[64,16,128]{2,1,0:T(8,128)(2,1)S(1)} custom-call(s32[1]{0:T(128)} %bitcast.refs_0_, s16[8,400,128]{2,1,0:T(8,128)(2,1)S(1)} %all-to-all-done.refs_1_, bf16[512,1024]{1,0:T(8,128)(2,1)S(1)} %pick.1.refs_2_), custom_call_target="tpu_custom_call" | custom-call | tf_op jit(solution)/shard_map/table/pallas_call | solution.py:234
  29.9 23.5 %all_to_all.15.in_ref = bf16[64,16,128]{2,1,0:T(8,128)(2,1)S(1)} all-to-all(bf16[64,16,128]{2,1,0:T(8,128)(2,1)S(1)} %table.1), channel_id=1, replica_groups=mesh['x'=4,'zh'=4,'y'=8,'zl'=2,'c'=2] {'zh','y','zl'}, dimensions={0} | all-to-all | bytes 524288 | tf_op jit(solution)/shard_map/all_to_all | solution.py:279
  53.3 0.1 sum.1
  53.4 10.1 %all_to_all.16.in_ref = f32[8,2,128]{2,1,0:T(2,128)S(1)} all-to-all(f32[8,2,128]{2,1,0:T(2,128)S(1)} %sum.1), channel_id=1, replica_groups=mesh['x'=4,'zh'=4,'y'=8,'zl'=2,'c'=2] {'x','c'}, dimensions={0} | all-to-all | bytes 16384 | tf_op jit(solution)/shard_map/all_to_all | solution.py:288
  63.5 0.0 copy-done
  63.5 0.0 copy-done.1
  63.5 0.0 copy-done.2
  63.5 0.8 %inverse.1 = f32[1,2,1024]{2,1,0:T(2,128)} custom-call(f32[8,2,128]{2,1,0:T(2,128)S(1)} %all_to_all.16.in_ref, bf16[384,256]{1,0:T(8,128)(2,1)S(1)} %copy-done, f32[2,16,128]{2,1,0:T(8,128)S(1)} %copy-done.2, f32[2,8,8,128]{3,2,1,0:T(8,128)S(1)} %copy-done.1), custom_call_target="tpu_custom_call" | custom-call | tf_op jit(solution)/shard_map/inverse/pallas_call | solution.py:291
  (1 shorter events, 0.0 us)
Async XLA Ops:
  0.0 13.9 %copy-start.3 = (s32[512]{0:T(512)S(1)}, s32[512]{0:T(512)}, u32[]{:S(2)}) copy-start(s32[512]{0:T(512)} %param.13) | copy-start | bytes 6148
  0.0 13.9 %copy-start.4 = (s32[512]{0:T(512)S(1)}, s32[512]{0:T(512)}, u32[]{:S(2)}) copy-start(s32[512]{0:T(512)} %param.14) | copy-start | bytes 6148
  3.4 60.1 %copy-start = (bf16[384,256]{1,0:T(8,128)(2,1)S(1)}, bf16[384,256]{1,0:T(8,128)(2,1)}, u32[]{:S(2)}) copy-start(bf16[384,256]{1,0:T(8,128)(2,1)} %constant.20.clone.main_ref) | copy-start | bytes 589828
  3.4 60.0 %copy-start.1 = (f32[2,8,8,128]{3,2,1,0:T(8,128)S(1)}, f32[2,8,8,128]{3,2,1,0:T(8,128)}, u32[]{:S(2)}) copy-start(f32[2,8,8,128]{3,2,1,0:T(8,128)} %constant.22.clone.last_ref) | copy-start | bytes 196612
  3.5 60.0 %copy-start.2 = (f32[2,16,128]{2,1,0:T(8,128)S(1)}, f32[2,16,128]{2,1,0:T(8,128)}, u32[]{:S(2)}) copy-start(f32[2,16,128]{2,1,0:T(8,128)} %constant.21.clone.twist_ref) | copy-start | bytes 49156
  3.5 23.1 %all-to-all-start = ((s16[8,400,128]{2,1,0:T(8,128)(2,1)}), s16[8,400,128]{2,1,0:T(8,128)(2,1)S(1)}, u32[]{:S(2)}, u32[]{:S(2)}) async-start(s16[8,400,128]{2,1,0:T(8,128)(2,1)} %merge.1), calls=%async_computation | async-start | bytes 1638400 | tf_op jit(solution)/shard_map/all_to_all | solution.py:263

commit v4 on v3

--- a/solution.py
+++ b/solution.py
@@ -18,7 +18,6 @@
 LEAST = 4e-34
 F32, BF16, I32, I16 = jnp.float32, jnp.bfloat16, jnp.int32, jnp.int16
 VMEM = 48 * 1024 * 1024
-MERGE_VMEM = 63 * 1024 * 1024
 
 
 def cos_sin(steps, samples):
@@ -27,8 +26,8 @@
     rest = steps - quadrant * (samples // 4)
     t = rest.astype(F32) * (2.0 * math.pi / samples)
     t2 = t * t
-    sine = t + t * t2 * (-1.0 / 6 + t2 * (1.0 / 120 + t2 * (-1.0 / 5040 + t2 * (1.0 / 362880))))
-    cosine = 1.0 + t2 * (-0.5 + t2 * (1.0 / 24 + t2 * (-1.0 / 720 + t2 * (1.0 / 40320))))
+    sine = t + t * t2 * (-1.0 / 6 + t2 * (1.0 / 120 + t2 * (-1.0 / 5040)))
+    cosine = 1.0 + t2 * (-0.5 + t2 * (1.0 / 24 + t2 * (-1.0 / 720)))
     odd = (quadrant & 1) == 1
     c = jnp.where(odd, sine, cosine)
     s = jnp.where(odd, cosine, sine)
@@ -37,7 +36,7 @@
     return c, s
 
 
-def merge_kernel(groups, green_ref, mech_ref, slip_ref, onset_ref, out_ref, green, mech, slip, onset, merged, msg, sems, out_sems):
+def merge_kernel(groups, green_ref, mech_ref, slip_ref, onset_ref, msg_ref, green, mech, slip, onset, merged, sems):
     _, comps, kinds, subs, freqs = green_ref.shape
     share = freqs // groups
     end = 2 * comps * share
@@ -51,7 +50,7 @@
         copy.start()
     copies[0].wait()
     cols = [jnp.broadcast_to(mech[k : k + 1, :], (subs, subs)).T for k in range(kinds)]
-    powers, sends = [], []
+    powers = []
     for i in range(2 * comps):
         copies[1 + i].wait()
         top = jnp.zeros((8, subs), F32)
@@ -70,25 +69,16 @@
         lines = slice(i * share, (i + 1) * share)
         for g in range(groups):
             part = merged[i, pl.ds(g, share, stride=groups), :] * inverse
-            msg[g, lines, :] = jnp.round(part).astype(I32).astype(I16)
-        sends.append(pltpu.make_async_copy(msg.at[:, lines], out_ref.at[:, lines], out_sems.at[i]))
-        sends[-1].start()
+            msg_ref[g, lines, :] = jnp.round(part).astype(I32).astype(I16)
         if i == 0:
             copies[-2].wait()
             codes = (slip[...].astype(F32) * SLIP_UNIT).astype(I32).astype(I16)
             for g in range(groups):
-                msg[g, end + 16 :, :] = codes
-            tail = slice(end + 16, msg.shape[1])
-            sends.append(pltpu.make_async_copy(msg.at[:, tail], out_ref.at[:, tail], out_sems.at[2 * comps]))
-            sends[-1].start()
+                msg_ref[g, end + 16 :, :] = codes
     copies[-1].wait()
     head = jnp.concatenate([jnp.broadcast_to(p, (8 // len(powers), subs)) for p in powers] + [onset[...]], axis=0).astype(I16)
     for g in range(groups):
-        msg[g, end : end + 16, :] = head
-    sends.append(pltpu.make_async_copy(msg.at[:, end : end + 16], out_ref.at[:, end : end + 16], out_sems.at[2 * comps + 1]))
-    sends[-1].start()
-    for send in sends:
-        send.wait()
+        msg_ref[g, end : end + 16, :] = head
 
 
 def pick_kernel(combo_ref, pick_ref):
@@ -98,7 +88,7 @@
         pick_ref[:, first : first + 128] = jnp.where(combo_ref[...] == ids, 1.0, 0.0).astype(BF16)
 
 
-def table_kernel(groups, samples, place_ref, msg_ref, pick_ref, out_ref, slips, values, shifted, turns, table):
+def table_kernel(groups, samples, place_ref, msg_ref, pick_ref, out_ref, slips, values, shifted, turns, table, onsets):
     hypos, _, rows = shifted.shape
     subs = values.shape[2]
     pats = slips.shape[0]
@@ -115,36 +105,48 @@
             lines = slice(i * share, (i + 1) * share)
             unit = jnp.exp2(head[2 * i : 2 * i + 1].astype(F32))
             values[src, lines, :] = msg_ref[src, lines, :].astype(I32).astype(F32) * unit
+        onsets[src] = head[8:16]
         near_c, near_s = cos_sin((head[8:16] * (8 * groups)) & (samples - 1), samples)
         turns[src, 0] = near_c
         turns[src, 1] = near_s
-        turns[src, 2] = near_c * near_c - near_s * near_s
-        turns[src, 3] = 2.0 * near_c * near_s
+        far_c, far_s = near_c * near_c - near_s * near_s, 2.0 * near_c * near_s
+        twice_c, twice_s = far_c * far_c - far_s * far_s, 2.0 * far_c * far_s
+        turns[src, 2], turns[src, 3] = far_c, far_s
+        turns[src, 4], turns[src, 5] = twice_c, twice_s
+        turns[src, 6], turns[src, 7] = far_c * twice_c - far_s * twice_s, far_c * twice_s + far_s * twice_c
 
     spectra = None
+    batch = 2
     for h in range(hypos):
-        for src in range(groups):
-            lanes = slice(src * subs, (src + 1) * subs)
-            onset = jnp.broadcast_to(msg_ref[src, rows : rows + 16, :].astype(I32)[8 + h : 9 + h], (8, subs))
-            c0, s0 = cos_sin((onset * freq) & (samples - 1), samples)
-            nc, ns = turns[src, 0, h : h + 1, :], turns[src, 1, h : h + 1, :]
-            c = jnp.concatenate([c0, c0 * nc - s0 * ns], axis=0)
-            s = jnp.concatenate([s0, s0 * nc + c0 * ns], axis=0)
-            jc = jnp.broadcast_to(turns[src, 2, h : h + 1, :], (16, subs))
-            js = jnp.broadcast_to(turns[src, 3, h : h + 1, :], (16, subs))
+        for first in range(0, groups, batch):
+            some = slice(first, first + batch)
+            onset = jnp.concatenate([jnp.broadcast_to(onsets[src, h : h + 1, :], (8, subs)) for src in range(first, first + batch)], axis=0)
+            c0, s0 = cos_sin((onset * jnp.concatenate([freq] * batch, axis=0)) & (samples - 1), samples)
+            c0, s0 = c0.reshape(batch, 8, subs), s0.reshape(batch, 8, subs)
+
+            def turned(pair, step):
+                jc, js = turns[some, 2 * step, h : h + 1, :], turns[some, 2 * step + 1, h : h + 1, :]
+                return pair[0] * jc - pair[1] * js, pair[1] * jc + pair[0] * js
+
+            low = [(c0, s0), turned((c0, s0), 0)]
             real, imag = [[], []], [[], []]
             for a in range(share // 16):
-                if a:
-                    c, s = c * jc - s * js, s * jc + c * js
+                now = [turned(pair, a) for pair in low] if a else low
                 for comp in range(2):
-                    r0 = comp * 2 * share + a * 16
-                    re = values[src, r0 : r0 + 16, :]
-                    im = values[src, r0 + share : r0 + share + 16, :]
-                    real[comp].append((c * re + s * im).astype(BF16))
-                    imag[comp].append((c * im - s * re).astype(BF16))
+                    re_out, im_out = [], []
+                    for half in range(2):
+                        c, s = now[half]
+                        r0 = comp * 2 * share + a * 16 + half * 8
+                        re = values[some, r0 : r0 + 8, :]
+                        im = values[some, r0 + share : r0 + share + 8, :]
+                        re_out.append(c * re + s * im)
+                        im_out.append(c * im - s * re)
+                    real[comp].append(jnp.concatenate(re_out, axis=1).astype(BF16))
+                    imag[comp].append(jnp.concatenate(im_out, axis=1).astype(BF16))
             for comp in range(2):
-                block = jnp.concatenate(real[comp] + imag[comp], axis=0).T
-                shifted[h, lanes, comp * 2 * share : (comp + 1) * 2 * share] = block.astype(BF16)
+                block = jnp.concatenate(real[comp] + imag[comp], axis=1)
+                for src in range(first, first + batch):
+                    shifted[h, src * subs : (src + 1) * subs, comp * 2 * share : (comp + 1) * 2 * share] = block[src - first].T
         sums = jnp.dot(slips[...], shifted[h], preferred_element_type=F32)
         sums = sums.astype(BF16)
         table[h * pats : (h + 1) * pats, :] = sums
@@ -211,20 +213,18 @@
         lambda *refs: merge_kernel(groups, *refs),
         out_shape=jax.ShapeDtypeStruct((groups, lines, subs), I16),
         in_specs=[pl.BlockSpec(memory_space=pltpu.HBM)] * 4,
-        out_specs=pl.BlockSpec(memory_space=pltpu.HBM),
+        out_specs=pl.BlockSpec(memory_space=pltpu.VMEM),
         scratch_shapes=[
             pltpu.VMEM((2 * comps, kinds, subs, freqs), BF16),
             pltpu.VMEM((kinds, subs), F32),
             pltpu.VMEM((pats, subs), BF16),
             pltpu.VMEM((hypos, subs), I32),
             pltpu.VMEM((2 * comps, freqs, subs), F32),
-            pltpu.VMEM((groups, lines, subs), I16),
             pltpu.SemaphoreType.DMA((2 * comps + 3,)),
-            pltpu.SemaphoreType.DMA((2 * comps + 2,)),
         ],
-        compiler_params=pltpu.CompilerParams(vmem_limit_bytes=MERGE_VMEM),
+        compiler_params=pltpu.CompilerParams(vmem_limit_bytes=VMEM),
         name="merge",
-    )(green, mechanism, slip, onset)
+    )(*(pltpu.with_memory_space_constraint(v, pltpu.HBM) for v in (green, mechanism, slip, onset)))
 
 
 def table_call(groups, samples, planes, hypos, pats, place, msg, pick):
@@ -240,8 +240,9 @@
             pltpu.VMEM((pats, groups * subs), BF16),
             pltpu.VMEM((groups, rows, subs), F32),
             pltpu.VMEM((hypos, groups * subs, rows), BF16),
-            pltpu.VMEM((groups, 4, hypos, subs), F32),
+            pltpu.VMEM((groups, 8, hypos, subs), F32),
             pltpu.VMEM((hypos * pats, rows), BF16),
+            pltpu.VMEM((groups, hypos, subs), I32),
         ],
         compiler_params=pltpu.CompilerParams(vmem_limit_bytes=VMEM),
         name="table",

time: 64.5 us -> 64.6 us (level)
  no operation moved by 1% of the time
where the time goes in v4:
time: 64.6 us; the launch traced here: 64.3 us
  blocking collectives  33.5 us (52%)
  waiting for transfers between devices  11.6 us (18%)
  starting transfers between devices  10.5 us (16%)
  Pallas kernels  8.23 us (13%)
    all_to_all x1, blocking collectives, on_device(): parts = lax.all_to_all(parts, PLANE, 0, 0, tiled=True)  23.5 us
    all_to_all x1, waiting for transfers between devices, on_device(): msg = lax.all_to_all(msg, GROUP, 0, 0, tiled=True)  11.6 us
    all_to_all x1, starting transfers between devices, on_device(): msg = lax.all_to_all(msg, GROUP, 0, 0, tiled=True)  10.5 us
    all_to_all x1, blocking collectives, on_device(): spectra = lax.all_to_all(summed, GROUP, 0, 0, tiled=True)  10.1 us
    pallas_call x1, Pallas kernels, merge_call(): pl.pallas_call(lambda *refs: merge_kernel(groups, *refs), out_shape=jax.S...  3.58 us
    pallas_call x1, Pallas kernels, table_call(): pl.pallas_call(lambda *refs: table_kernel(groups, samples, *refs), out_sh...  3.2 us
  transfers between devices with their start and end apart: 1, of which 1 were waited for; matrix products, arithmetic and copies ran while one was open for 1% of the time, Pallas kernels for 1%

profile of v4, /device:TPU:1, one launch (start us, length us, event | category | flops | bytes accessed | tf_op | source)
XLA Modules:
  0.0 64.3 jit_solution(4886986209197856603)
XLA Ops:
  0.0 0.0 copy-start.3
  0.0 0.0 copy-start.4
  0.0 3.6 %merge.1 = s16[8,400,128]{2,1,0:T(8,128)(2,1)} custom-call(bf16[2,2,6,128,512]{4,3,2,1,0:T(8,128)(2,1)} %refs_0_.1, f32[6,128]{1,0:T(8,128)} %refs_1_.1, bf16[128,128]{1,0:T(8,128)(2,1)} %refs_2_.1, s32[8,128]{1,0:T(8,128)} %refs_3_.1), custom_call_target="tpu_custom_call" | custom-call | tf_op jit(solution)/shard_map/merge/pallas_call | solution.py:212
  3.6 0.0 copy-start
  3.6 0.0 copy-start.1
  3.6 0.0 copy-start.2
  3.6 10.5 %all-to-all-start = ((s16[8,400,128]{2,1,0:T(8,128)(2,1)}), s16[8,400,128]{2,1,0:T(8,128)(2,1)S(1)}, u32[]{:S(2)}, u32[]{:S(2)}) async-start(s16[8,400,128]{2,1,0:T(8,128)(2,1)} %merge.1), calls=%async_computation | async-start | bytes 1638400 | tf_op jit(solution)/shard_map/all_to_all | solution.py:264
  14.1 0.0 copy-done.3
  14.1 0.0 copy-done.4
  14.1 0.1 reshape.10
  14.3 0.1 copy.10
  14.4 0.1 reshape.12.combo_ref
  14.5 0.6 pick.1.refs_2_
  15.1 11.6 %all-to-all-done.refs_1_ = s16[8,400,128]{2,1,0:T(8,128)(2,1)S(1)} async-done(((s16[8,400,128]{2,1,0:T(8,128)(2,1)}), s16[8,400,128]{2,1,0:T(8,128)(2,1)S(1)}, u32[]{:S(2)}, u32[]{:S(2)}) %all-to-all-start) | async-done | bytes 819232 | tf_op jit(solution)/shard_map/all_to_all | solution.py:264
  26.8 3.2 %table.1 = bf16[64,16,128]{2,1,0:T(8,128)(2,1)S(1)} custom-call(s32[1]{0:T(128)} %bitcast.refs_0_, s16[8,400,128]{2,1,0:T(8,128)(2,1)S(1)} %all-to-all-done.refs_1_, bf16[512,1024]{1,0:T(8,128)(2,1)S(1)} %pick.1.refs_2_), custom_call_target="tpu_custom_call" | custom-call | tf_op jit(solution)/shard_map/table/pallas_call | solution.py:234
  30.0 23.5 %all_to_all.15.in_ref = bf16[64,16,128]{2,1,0:T(8,128)(2,1)S(1)} all-to-all(bf16[64,16,128]{2,1,0:T(8,128)(2,1)S(1)} %table.1), channel_id=1, replica_groups=mesh['x'=4,'zh'=4,'y'=8,'zl'=2,'c'=2] {'zh','y','zl'}, dimensions={0} | all-to-all | bytes 524288 | tf_op jit(solution)/shard_map/all_to_all | solution.py:280
  53.4 0.1 sum.1
  53.5 10.1 %all_to_all.16.in_ref = f32[8,2,128]{2,1,0:T(2,128)S(1)} all-to-all(f32[8,2,128]{2,1,0:T(2,128)S(1)} %sum.1), channel_id=1, replica_groups=mesh['x'=4,'zh'=4,'y'=8,'zl'=2,'c'=2] {'x','c'}, dimensions={0} | all-to-all | bytes 16384 | tf_op jit(solution)/shard_map/all_to_all | solution.py:289
  63.6 0.0 copy-done
  63.6 0.0 copy-done.1
  63.6 0.0 copy-done.2
  63.6 0.8 %inverse.1 = f32[1,2,1024]{2,1,0:T(2,128)} custom-call(f32[8,2,128]{2,1,0:T(2,128)S(1)} %all_to_all.16.in_ref, bf16[384,256]{1,0:T(8,128)(2,1)S(1)} %copy-done, f32[2,16,128]{2,1,0:T(8,128)S(1)} %copy-done.2, f32[2,8,8,128]{3,2,1,0:T(8,128)S(1)} %copy-done.1), custom_call_target="tpu_custom_call" | custom-call | tf_op jit(solution)/shard_map/inverse/pallas_call | solution.py:292
  (1 shorter events, 0.0 us)
Async XLA Ops:
  0.0 14.1 %copy-start.3 = (s32[512]{0:T(512)S(1)}, s32[512]{0:T(512)}, u32[]{:S(2)}) copy-start(s32[512]{0:T(512)} %param.13) | copy-start | bytes 6148
  0.0 14.1 %copy-start.4 = (s32[512]{0:T(512)S(1)}, s32[512]{0:T(512)}, u32[]{:S(2)}) copy-start(s32[512]{0:T(512)} %param.14) | copy-start | bytes 6148
  3.6 60.0 %copy-start = (bf16[384,256]{1,0:T(8,128)(2,1)S(1)}, bf16[384,256]{1,0:T(8,128)(2,1)}, u32[]{:S(2)}) copy-start(bf16[384,256]{1,0:T(8,128)(2,1)} %constant.20.clone.main_ref) | copy-start | bytes 589828
  3.6 60.0 %copy-start.1 = (f32[2,8,8,128]{3,2,1,0:T(8,128)S(1)}, f32[2,8,8,128]{3,2,1,0:T(8,128)}, u32[]{:S(2)}) copy-start(f32[2,8,8,128]{3,2,1,0:T(8,128)} %constant.22.clone.last_ref) | copy-start | bytes 196612
  3.6 60.0 %copy-start.2 = (f32[2,16,128]{2,1,0:T(8,128)S(1)}, f32[2,16,128]{2,1,0:T(8,128)}, u32[]{:S(2)}) copy-start(f32[2,16,128]{2,1,0:T(8,128)} %constant.21.clone.twist_ref) | copy-start | bytes 49156
  3.6 23.1 %all-to-all-start = ((s16[8,400,128]{2,1,0:T(8,128)(2,1)}), s16[8,400,128]{2,1,0:T(8,128)(2,1)S(1)}, u32[]{:S(2)}, u32[]{:S(2)}) async-start(s16[8,400,128]{2,1,0:T(8,128)(2,1)} %merge.1), calls=%async_computation | async-start | bytes 1638400 | tf_op jit(solution)/shard_map/all_to_all | solution.py:264

commit v5 on v4

--- a/solution.py
+++ b/solution.py
@@ -36,7 +36,23 @@
     return c, s
 
 
-def merge_kernel(groups, green_ref, mech_ref, slip_ref, onset_ref, msg_ref, green, mech, slip, onset, merged, sems):
+def choose(groups, ring, pats, pattern, hypo, pick_ref, across, ordered):
+    count, entries = pick_ref.shape
+    pair = groups * ring // count
+    width = min(count, 128)
+    for first in range(0, count, width):
+        some = slice(first, first + width)
+        combo = hypo[some] * pats + pattern[some]
+        across[some, :] = jnp.broadcast_to(combo.reshape(1, width), (128, width)).T
+    for place in range(groups):
+        source = pl.ds(place // pair * ring + place % pair, count // groups, stride=pair)
+        ordered[pl.ds(place, count // groups, stride=groups), :] = across[source, :]
+    for first in range(0, entries, 128):
+        ids = lax.broadcasted_iota(I32, (count, 128), 1) + first
+        pick_ref[:, first : first + 128] = jnp.where(ordered[...] == ids, 1.0, 0.0).astype(BF16)
+
+
+def merge_kernel(groups, ring, pats, green_ref, mech_ref, slip_ref, onset_ref, pattern_ref, hypo_ref, msg_ref, pick_ref, green, mech, slip, onset, pattern, hypo, across, ordered, merged, sems):
     _, comps, kinds, subs, freqs = green_ref.shape
     share = freqs // groups
     end = 2 * comps * share
@@ -46,8 +62,15 @@
         copies.append(pltpu.make_async_copy(green_ref.at[q, c], green.at[i], sems.at[1 + i]))
     copies.append(pltpu.make_async_copy(slip_ref, slip, sems.at[1 + 2 * comps]))
     copies.append(pltpu.make_async_copy(onset_ref, onset, sems.at[2 + 2 * comps]))
-    for copy in copies:
+    rest = [
+        pltpu.make_async_copy(pattern_ref, pattern, sems.at[3 + 2 * comps]),
+        pltpu.make_async_copy(hypo_ref, hypo, sems.at[4 + 2 * comps]),
+    ]
+    for copy in rest + copies:
         copy.start()
+    for copy in rest:
+        copy.wait()
+    choose(groups, ring, pats, pattern, hypo, pick_ref, across, ordered)
     copies[0].wait()
     cols = [jnp.broadcast_to(mech[k : k + 1, :], (subs, subs)).T for k in range(kinds)]
     powers = []
@@ -76,24 +99,17 @@
             for g in range(groups):
                 msg_ref[g, end + 16 :, :] = codes
     copies[-1].wait()
-    head = jnp.concatenate([jnp.broadcast_to(p, (8 // len(powers), subs)) for p in powers] + [onset[...]], axis=0).astype(I16)
     for g in range(groups):
-        msg_ref[g, end : end + 16, :] = head
-
-
-def pick_kernel(combo_ref, pick_ref):
-    count, entries = pick_ref.shape
-    for first in range(0, entries, 128):
-        ids = lax.broadcasted_iota(I32, (count, 128), 1) + first
-        pick_ref[:, first : first + 128] = jnp.where(combo_ref[...] == ids, 1.0, 0.0).astype(BF16)
-
-
-def table_kernel(groups, samples, place_ref, msg_ref, pick_ref, out_ref, slips, values, shifted, turns, table, onsets):
+        rows = powers + [jnp.full((8 - len(powers), subs), g, I32), onset[...]]
+        msg_ref[g, end : end + 16, :] = jnp.concatenate(rows, axis=0).astype(I16)
+
+
+def table_kernel(groups, samples, msg_ref, pick_ref, out_ref, slips, values, shifted, turns, table, onsets):
     hypos, _, rows = shifted.shape
     subs = values.shape[2]
     pats = slips.shape[0]
     share = rows // 4
-    mine = place_ref[0]
+    mine = msg_ref[0, rows : rows + 16, :].astype(I32)[4:5]
     freq = mine + groups * lax.broadcasted_iota(I32, (8, subs), 0)
 
     for src in range(groups):
@@ -103,7 +119,7 @@
         head = msg_ref[src, rows : rows + 16, :].astype(I32)
         for i in range(4):
             lines = slice(i * share, (i + 1) * share)
-            unit = jnp.exp2(head[2 * i : 2 * i + 1].astype(F32))
+            unit = jnp.exp2(head[i : i + 1].astype(F32))
             values[src, lines, :] = msg_ref[src, lines, :].astype(I32).astype(F32) * unit
         onsets[src] = head[8:16]
         near_c, near_s = cos_sin((head[8:16] * (8 * groups)) & (samples - 1), samples)
@@ -205,36 +221,44 @@
             out_ref[0, comp : comp + 1, a * 128 : (a + 1) * 128] = total[a : a + 1]
 
 
-def merge_call(groups, green, mechanism, slip, onset):
+def merge_call(groups, ring, green, mechanism, slip, onset, pattern, hypo):
     _, comps, kinds, subs, freqs = green.shape
     pats, hypos = slip.shape[0], onset.shape[0]
     lines = 2 * comps * freqs // groups + 16 + pats
+    count = pattern.shape[0]
     return pl.pallas_call(
-        lambda *refs: merge_kernel(groups, *refs),
-        out_shape=jax.ShapeDtypeStruct((groups, lines, subs), I16),
-        in_specs=[pl.BlockSpec(memory_space=pltpu.HBM)] * 4,
-        out_specs=pl.BlockSpec(memory_space=pltpu.VMEM),
+        lambda *refs: merge_kernel(groups, ring, pats, *refs),
+        out_shape=(
+            jax.ShapeDtypeStruct((groups, lines, subs), I16),
+            jax.ShapeDtypeStruct((count, hypos * pats), BF16),
+        ),
+        in_specs=[pl.BlockSpec(memory_space=pltpu.HBM)] * 6,
+        out_specs=(pl.BlockSpec(memory_space=pltpu.VMEM),) * 2,
         scratch_shapes=[
             pltpu.VMEM((2 * comps, kinds, subs, freqs), BF16),
             pltpu.VMEM((kinds, subs), F32),
             pltpu.VMEM((pats, subs), BF16),
             pltpu.VMEM((hypos, subs), I32),
+            pltpu.VMEM((count,), I32),
+            pltpu.VMEM((count,), I32),
+            pltpu.VMEM((count, 128), I32),
+            pltpu.VMEM((count, 128), I32),
             pltpu.VMEM((2 * comps, freqs, subs), F32),
-            pltpu.SemaphoreType.DMA((2 * comps + 3,)),
+            pltpu.SemaphoreType.DMA((2 * comps + 5,)),
         ],
         compiler_params=pltpu.CompilerParams(vmem_limit_bytes=VMEM),
         name="merge",
-    )(*(pltpu.with_memory_space_constraint(v, pltpu.HBM) for v in (green, mechanism, slip, onset)))
-
-
-def table_call(groups, samples, planes, hypos, pats, place, msg, pick):
+    )(*(pltpu.with_memory_space_constraint(v, pltpu.HBM) for v in (green, mechanism, slip, onset, pattern, hypo)))
+
+
+def table_call(groups, samples, planes, hypos, pats, msg, pick):
     subs = msg.shape[2]
     rows = msg.shape[1] - 16 - pats
     in_vmem = pl.BlockSpec(memory_space=pltpu.VMEM)
     return pl.pallas_call(
         lambda *refs: table_kernel(groups, samples, *refs),
         out_shape=jax.ShapeDtypeStruct((planes, pick.shape[0] // planes * (rows // 128), 128), BF16),
-        in_specs=[pl.BlockSpec(memory_space=pltpu.SMEM), in_vmem, in_vmem],
+        in_specs=[in_vmem, in_vmem],
         out_specs=in_vmem,
         scratch_shapes=[
             pltpu.VMEM((pats, groups * subs), BF16),
@@ -246,7 +270,7 @@
         ],
         compiler_params=pltpu.CompilerParams(vmem_limit_bytes=VMEM),
         name="table",
-    )(place, msg, pick)
+    )(msg, pick)
 
 
 def on_device(green, mechanism, slip, onset, pattern_of_variation, hypo_of_variation):
@@ -258,24 +282,12 @@
     count = pattern_of_variation.shape[0]
     rows = 2 * comps * freqs // groups
     params = pltpu.CompilerParams(vmem_limit_bytes=VMEM)
-    in_vmem = pl.BlockSpec(memory_space=pltpu.VMEM)
-
-    msg = merge_call(groups, green, mechanism, slip, onset)
+
+    ring = count // lax.axis_size("x")
+    msg, pick = merge_call(groups, ring, green, mechanism, slip, onset, pattern_of_variation, hypo_of_variation)
     msg = lax.all_to_all(msg, GROUP, 0, 0, tiled=True)
 
-    combos = hypo_of_variation * pats + pattern_of_variation
-    gx, gc = lax.axis_size("x"), lax.axis_size("c")
-    combos = combos.reshape(gx, planes, gc).transpose(1, 0, 2).reshape(count, 1)
-    pick = pl.pallas_call(
-        pick_kernel,
-        out_shape=jax.ShapeDtypeStruct((count, hypos * pats), BF16),
-        in_specs=[in_vmem],
-        out_specs=in_vmem,
-        compiler_params=params,
-        name="pick",
-    )(combos)
-    place = lax.axis_index(GROUP).astype(I32).reshape(1)
-    parts = table_call(groups, samples, planes, hypos, pats, place, msg, pick)
+    parts = table_call(groups, samples, planes, hypos, pats, msg, pick)
 
     parts = lax.all_to_all(parts, PLANE, 0, 0, tiled=True)
 

time: 64.6 us -> 63.5 us (0.983)
  blocking collectives: 33.5 us -> 56.5 us
  waiting for transfers between devices: 11.6 us -> 0 us
  starting transfers between devices: 10.5 us -> 0 us
  Pallas kernels: 8.23 us -> 6.79 us
    all_to_all x0 -> x1, blocking collectives: none -> 22.3 us  [on_device(): msg = lax.all_to_all(msg, GROUP, 0, 0, tiled=True)]
    all_to_all x1 -> x0, waiting for transfers between devices: 11.6 us -> none  [on_device(): msg = lax.all_to_all(msg, GROUP, 0, 0, tiled=True)]
    all_to_all x1 -> x0, starting transfers between devices: 10.5 us -> none  [on_device(): msg = lax.all_to_all(msg, GROUP, 0, 0, tiled=True)]
    pallas_call x2 -> x1, Pallas kernels: 4.18 us -> 2.74 us  [merge_call(): pl.pallas_call(lambda *refs: merge_kernel(groups, ring, pats, *refs), out...]
    all_to_all x1, blocking collectives: 23.5 us -> 24.3 us  [on_device(): parts = lax.all_to_all(parts, PLANE, 0, 0, tiled=True)]
  transfers between devices with their start and end apart: 1 -> 0, of which waited for: 1 -> 0; matrix products, arithmetic and copies ran while one was open for 1% -> 0% of each run, Pallas kernels for 1% -> 0%
where the time goes in v5:
time: 63.5 us; the launch traced here: 63.3 us
  blocking collectives  56.5 us (89%)
  Pallas kernels  6.79 us (11%)
    all_to_all x1, blocking collectives, on_device(): parts = lax.all_to_all(parts, PLANE, 0, 0, tiled=True)  24.3 us
    all_to_all x1, blocking collectives, on_device(): msg = lax.all_to_all(msg, GROUP, 0, 0, tiled=True)  22.3 us
    all_to_all x1, blocking collectives, on_device(): spectra = lax.all_to_all(summed, GROUP, 0, 0, tiled=True)  9.84 us
    pallas_call x1, Pallas kernels, table_call(): pl.pallas_call(lambda *refs: table_kernel(groups, samples, *refs), out_sh...  3.2 us
    pallas_call x1, Pallas kernels, merge_call(): pl.pallas_call(lambda *refs: merge_kernel(groups, ring, pats, *refs), out...  2.74 us

profile of v5, /device:TPU:1, one launch (start us, length us, event | category | flops | bytes accessed | tf_op | source)
XLA Modules:
  0.0 63.3 jit_solution(647335041587680926)
XLA Ops:
  0.0 0.0 copy-start
  0.0 0.0 copy-start.1
  0.0 0.0 copy-start.2
  0.0 2.7 %merge.1 = (s16[8,400,128]{2,1,0:T(8,128)(2,1)S(1)}, bf16[512,1024]{1,0:T(8,128)(2,1)S(1)}) custom-call(bf16[2,2,6,128,512]{4,3,2,1,0:T(8,128)(2,1)} %refs_0_.1, f32[6,128]{1,0:T(8,128)} %refs_1_.1, bf16[128,128]{1,0:T(8,128)(2,1)} %refs_2_.1, s32[8,128]{1,0:T(8,128)} %refs_3_.1, s32[512]{0:T(512)} %refs_4_.1, s32[512]{0:T(512)} %refs_5_.1), custom_call_target="tpu_custom_call" | custom-call | tf_op jit(solution)/shard_map/merge/pallas_call | solution.py:229
  2.8 22.3 %all_to_all.15.refs_0_ = s16[8,400,128]{2,1,0:T(8,128)(2,1)S(1)} all-to-all(s16[8,400,128]{2,1,0:T(8,128)(2,1)S(1)} %get-tuple-element.7), channel_id=1, replica_groups=mesh['x'=4,'zh'=4,'y'=8,'zl'=2,'c'=2] {'x','c'}, dimensions={0} | all-to-all | bytes 1638400 | tf_op jit(solution)/shard_map/all_to_all | solution.py:288
  25.0 3.2 %table.1 = bf16[64,16,128]{2,1,0:T(8,128)(2,1)S(1)} custom-call(s16[8,400,128]{2,1,0:T(8,128)(2,1)S(1)} %all_to_all.15.refs_0_, bf16[512,1024]{1,0:T(8,128)(2,1)S(1)} %get-tuple-element.8.refs_1_), custom_call_target="tpu_custom_call" | custom-call | tf_op jit(solution)/shard_map/table/pallas_call | solution.py:258
  28.2 24.3 %all_to_all.16.in_ref = bf16[64,16,128]{2,1,0:T(8,128)(2,1)S(1)} all-to-all(bf16[64,16,128]{2,1,0:T(8,128)(2,1)S(1)} %table.1), channel_id=1, replica_groups=mesh['x'=4,'zh'=4,'y'=8,'zl'=2,'c'=2] {'zh','y','zl'}, dimensions={0} | all-to-all | bytes 524288 | tf_op jit(solution)/shard_map/all_to_all | solution.py:292
  52.6 0.1 sum.1
  52.7 9.8 %all_to_all.17.in_ref = f32[8,2,128]{2,1,0:T(2,128)S(1)} all-to-all(f32[8,2,128]{2,1,0:T(2,128)S(1)} %sum.1), channel_id=1, replica_groups=mesh['x'=4,'zh'=4,'y'=8,'zl'=2,'c'=2] {'x','c'}, dimensions={0} | all-to-all | bytes 16384 | tf_op jit(solution)/shard_map/all_to_all | solution.py:301
  62.5 0.0 copy-done
  62.5 0.0 copy-done.1
  62.5 0.0 copy-done.2
  62.5 0.8 %inverse.1 = f32[1,2,1024]{2,1,0:T(2,128)} custom-call(f32[8,2,128]{2,1,0:T(2,128)S(1)} %all_to_all.17.in_ref, bf16[384,256]{1,0:T(8,128)(2,1)S(1)} %copy-done, f32[2,16,128]{2,1,0:T(8,128)S(1)} %copy-done.2, f32[2,8,8,128]{3,2,1,0:T(8,128)S(1)} %copy-done.1), custom_call_target="tpu_custom_call" | custom-call | tf_op jit(solution)/shard_map/inverse/pallas_call | solution.py:304
Async XLA Ops:
  0.0 62.5 %copy-start = (bf16[384,256]{1,0:T(8,128)(2,1)S(1)}, bf16[384,256]{1,0:T(8,128)(2,1)}, u32[]{:S(2)}) copy-start(bf16[384,256]{1,0:T(8,128)(2,1)} %constant.6.clone.main_ref) | copy-start | bytes 589828
  0.0 62.5 %copy-start.1 = (f32[2,8,8,128]{3,2,1,0:T(8,128)S(1)}, f32[2,8,8,128]{3,2,1,0:T(8,128)}, u32[]{:S(2)}) copy-start(f32[2,8,8,128]{3,2,1,0:T(8,128)} %constant.8.clone.last_ref) | copy-start | bytes 196612
  0.0 62.5 %copy-start.2 = (f32[2,16,128]{2,1,0:T(8,128)S(1)}, f32[2,16,128]{2,1,0:T(8,128)}, u32[]{:S(2)}) copy-start(f32[2,16,128]{2,1,0:T(8,128)} %constant.7.clone.twist_ref) | copy-start | bytes 49156

commit v6 on v5

--- a/solution.py
+++ b/solution.py
@@ -66,16 +66,20 @@
         pltpu.make_async_copy(pattern_ref, pattern, sems.at[3 + 2 * comps]),
         pltpu.make_async_copy(hypo_ref, hypo, sems.at[4 + 2 * comps]),
     ]
-    for copy in rest + copies:
+    for copy in rest + copies[:1] + copies[-2:] + copies[1:-2]:
         copy.start()
     for copy in rest:
         copy.wait()
     choose(groups, ring, pats, pattern, hypo, pick_ref, across, ordered)
+    copies[-2].wait()
+    codes = (slip[...].astype(F32) * SLIP_UNIT).astype(I32).astype(I16)
+    for g in range(groups):
+        msg_ref[g, end + 16 :, :] = codes
     copies[0].wait()
     cols = [jnp.broadcast_to(mech[k : k + 1, :], (subs, subs)).T for k in range(kinds)]
     powers = []
-    for i in range(2 * comps):
-        copies[1 + i].wait()
+
+    def merge(i):
         top = jnp.zeros((8, subs), F32)
         for tile in range(freqs // subs):
             piece = slice(tile * subs, (tile + 1) * subs)
@@ -85,6 +89,9 @@
             total = total.T
             merged[i, piece, :] = total
             top = jnp.maximum(top, jnp.max(jnp.abs(total).reshape(subs // 8, 8, subs), axis=0))
+        return top
+
+    def encode(i, top):
         most = jnp.maximum(jnp.max(top, axis=0, keepdims=True), LEAST)
         power = jnp.maximum(jnp.ceil(jnp.log2(most * (1.0 / CODE_TOP))), -126.0)
         powers.append(power.astype(I32))
@@ -93,11 +100,14 @@
         for g in range(groups):
             part = merged[i, pl.ds(g, share, stride=groups), :] * inverse
             msg_ref[g, lines, :] = jnp.round(part).astype(I32).astype(I16)
-        if i == 0:
-            copies[-2].wait()
-            codes = (slip[...].astype(F32) * SLIP_UNIT).astype(I32).astype(I16)
-            for g in range(groups):
-                msg_ref[g, end + 16 :, :] = codes
+
+    for i in range(2 * comps):
+        copies[1 + i].wait()
+        top = merge(i)
+        if i:
+            encode(i - 1, before)
+        before = top
+    encode(2 * comps - 1, before)
     copies[-1].wait()
     for g in range(groups):
         rows = powers + [jnp.full((8 - len(powers), subs), g, I32), onset[...]]

time: 63.5 us -> 63.3 us (level)
  no operation moved by 1% of the time
where the time goes in v6:
time: 63.3 us; the launch traced here: 63.1 us
  blocking collectives  56.5 us (89%)
  Pallas kernels  6.57 us (10%)
    all_to_all x1, blocking collectives, on_device(): parts = lax.all_to_all(parts, PLANE, 0, 0, tiled=True)  24.3 us
    all_to_all x1, blocking collectives, on_device(): msg = lax.all_to_all(msg, GROUP, 0, 0, tiled=True)  22.3 us
    all_to_all x1, blocking collectives, on_device(): spectra = lax.all_to_all(summed, GROUP, 0, 0, tiled=True)  9.84 us
    pallas_call x1, Pallas kernels, table_call(): pl.pallas_call(lambda *refs: table_kernel(groups, samples, *refs), out_sh...  3.2 us
    pallas_call x1, Pallas kernels, merge_call(): pl.pallas_call(lambda *refs: merge_kernel(groups, ring, pats, *refs), out...  2.52 us

profile of v6, /device:TPU:1, one launch (start us, length us, event | category | flops | bytes accessed | tf_op | source)
XLA Modules:
  0.0 63.1 jit_solution(7107276473032290929)
XLA Ops:
  0.0 0.0 copy-start
  0.0 0.0 copy-start.1
  0.0 0.0 copy-start.2
  0.0 2.5 %merge.1 = (s16[8,400,128]{2,1,0:T(8,128)(2,1)S(1)}, bf16[512,1024]{1,0:T(8,128)(2,1)S(1)}) custom-call(bf16[2,2,6,128,512]{4,3,2,1,0:T(8,128)(2,1)} %refs_0_.1, f32[6,128]{1,0:T(8,128)} %refs_1_.1, bf16[128,128]{1,0:T(8,128)(2,1)} %refs_2_.1, s32[8,128]{1,0:T(8,128)} %refs_3_.1, s32[512]{0:T(512)} %refs_4_.1, s32[512]{0:T(512)} %refs_5_.1), custom_call_target="tpu_custom_call" | custom-call | tf_op jit(solution)/shard_map/merge/pallas_call | solution.py:239
  2.5 22.3 %all_to_all.15.refs_0_ = s16[8,400,128]{2,1,0:T(8,128)(2,1)S(1)} all-to-all(s16[8,400,128]{2,1,0:T(8,128)(2,1)S(1)} %get-tuple-element.7), channel_id=1, replica_groups=mesh['x'=4,'zh'=4,'y'=8,'zl'=2,'c'=2] {'x','c'}, dimensions={0} | all-to-all | bytes 1638400 | tf_op jit(solution)/shard_map/all_to_all | solution.py:298
  24.8 3.2 %table.1 = bf16[64,16,128]{2,1,0:T(8,128)(2,1)S(1)} custom-call(s16[8,400,128]{2,1,0:T(8,128)(2,1)S(1)} %all_to_all.15.refs_0_, bf16[512,1024]{1,0:T(8,128)(2,1)S(1)} %get-tuple-element.8.refs_1_), custom_call_target="tpu_custom_call" | custom-call | tf_op jit(solution)/shard_map/table/pallas_call | solution.py:268
  28.0 24.3 %all_to_all.16.in_ref = bf16[64,16,128]{2,1,0:T(8,128)(2,1)S(1)} all-to-all(bf16[64,16,128]{2,1,0:T(8,128)(2,1)S(1)} %table.1), channel_id=1, replica_groups=mesh['x'=4,'zh'=4,'y'=8,'zl'=2,'c'=2] {'zh','y','zl'}, dimensions={0} | all-to-all | bytes 524288 | tf_op jit(solution)/shard_map/all_to_all | solution.py:302
  52.4 0.1 sum.1
  52.4 9.8 %all_to_all.17.in_ref = f32[8,2,128]{2,1,0:T(2,128)S(1)} all-to-all(f32[8,2,128]{2,1,0:T(2,128)S(1)} %sum.1), channel_id=1, replica_groups=mesh['x'=4,'zh'=4,'y'=8,'zl'=2,'c'=2] {'x','c'}, dimensions={0} | all-to-all | bytes 16384 | tf_op jit(solution)/shard_map/all_to_all | solution.py:311
  62.3 0.0 copy-done
  62.3 0.0 copy-done.1
  62.3 0.0 copy-done.2
  62.3 0.8 %inverse.1 = f32[1,2,1024]{2,1,0:T(2,128)} custom-call(f32[8,2,128]{2,1,0:T(2,128)S(1)} %all_to_all.17.in_ref, bf16[384,256]{1,0:T(8,128)(2,1)S(1)} %copy-done, f32[2,16,128]{2,1,0:T(8,128)S(1)} %copy-done.2, f32[2,8,8,128]{3,2,1,0:T(8,128)S(1)} %copy-done.1), custom_call_target="tpu_custom_call" | custom-call | tf_op jit(solution)/shard_map/inverse/pallas_call | solution.py:314
Async XLA Ops:
  0.0 62.3 %copy-start = (bf16[384,256]{1,0:T(8,128)(2,1)S(1)}, bf16[384,256]{1,0:T(8,128)(2,1)}, u32[]{:S(2)}) copy-start(bf16[384,256]{1,0:T(8,128)(2,1)} %constant.6.clone.main_ref) | copy-start | bytes 589828
  0.0 62.3 %copy-start.1 = (f32[2,8,8,128]{3,2,1,0:T(8,128)S(1)}, f32[2,8,8,128]{3,2,1,0:T(8,128)}, u32[]{:S(2)}) copy-start(f32[2,8,8,128]{3,2,1,0:T(8,128)} %constant.8.clone.last_ref) | copy-start | bytes 196612
  0.0 62.3 %copy-start.2 = (f32[2,16,128]{2,1,0:T(8,128)S(1)}, f32[2,16,128]{2,1,0:T(8,128)}, u32[]{:S(2)}) copy-start(f32[2,16,128]{2,1,0:T(8,128)} %constant.7.clone.twist_ref) | copy-start | bytes 49156

commit v7 on v6

--- a/solution.py
+++ b/solution.py
@@ -12,7 +12,6 @@
 
 AXES = ("x", "zh", "y", "zl", "c")
 GROUP = ("x", "c")
-PLANE = ("zh", "y", "zl")
 CODE_TOP = 32000.0
 SLIP_UNIT = 2048.0
 LEAST = 4e-34
@@ -36,23 +35,19 @@
     return c, s
 
 
-def choose(groups, ring, pats, pattern, hypo, pick_ref, across, ordered):
+def choose(pats, pattern, hypo, pick_ref, across):
     count, entries = pick_ref.shape
-    pair = groups * ring // count
     width = min(count, 128)
     for first in range(0, count, width):
         some = slice(first, first + width)
         combo = hypo[some] * pats + pattern[some]
         across[some, :] = jnp.broadcast_to(combo.reshape(1, width), (128, width)).T
-    for place in range(groups):
-        source = pl.ds(place // pair * ring + place % pair, count // groups, stride=pair)
-        ordered[pl.ds(place, count // groups, stride=groups), :] = across[source, :]
     for first in range(0, entries, 128):
         ids = lax.broadcasted_iota(I32, (count, 128), 1) + first
-        pick_ref[:, first : first + 128] = jnp.where(ordered[...] == ids, 1.0, 0.0).astype(BF16)
-
-
-def merge_kernel(groups, ring, pats, green_ref, mech_ref, slip_ref, onset_ref, pattern_ref, hypo_ref, msg_ref, pick_ref, green, mech, slip, onset, pattern, hypo, across, ordered, merged, sems):
+        pick_ref[:, first : first + 128] = jnp.where(across[...] == ids, 1.0, 0.0).astype(BF16)
+
+
+def merge_kernel(groups, pats, green_ref, mech_ref, slip_ref, onset_ref, pattern_ref, hypo_ref, msg_ref, pick_ref, green, mech, slip, onset, pattern, hypo, across, merged, sems):
     _, comps, kinds, subs, freqs = green_ref.shape
     share = freqs // groups
     end = 2 * comps * share
@@ -70,7 +65,7 @@
         copy.start()
     for copy in rest:
         copy.wait()
-    choose(groups, ring, pats, pattern, hypo, pick_ref, across, ordered)
+    choose(pats, pattern, hypo, pick_ref, across)
     copies[-2].wait()
     codes = (slip[...].astype(F32) * SLIP_UNIT).astype(I32).astype(I16)
     for g in range(groups):
@@ -177,17 +172,7 @@
         sums = sums.astype(BF16)
         table[h * pats : (h + 1) * pats, :] = sums
     spectra = jnp.dot(pick_ref[...], table[...], preferred_element_type=F32)
-    dests = out_ref.shape[0]
-    parts = [spectra[:, i : i + 128].reshape(dests, -1, 128) for i in range(0, rows, 128)]
-    out_ref[...] = jnp.concatenate(parts, axis=1).astype(BF16)
-
-
-def sum_kernel(in_ref, out_ref):
-    total = jnp.sum(in_ref[...].astype(F32), axis=0)
-    rows = out_ref.shape[0]
-    for i in range(rows):
-        for half in range(2):
-            out_ref[i, half : half + 1, :] = total[half * rows + i : half * rows + i + 1, :]
+    out_ref[...] = spectra.reshape(out_ref.shape).astype(BF16)
 
 
 def inverse_tables(groups, freqs, samples):
@@ -208,9 +193,16 @@
     return [main, twist.astype(np.float32), last.astype(np.float32)]
 
 
-def inverse_kernel(in_ref, main_ref, twist_ref, last_ref, out_ref):
-    groups, comps, width = in_ref.shape
-    rows = jnp.concatenate([in_ref[:, comp, :] for comp in range(comps)], axis=0)
+def inverse_kernel(rings, pair, in_ref, main_ref, twist_ref, last_ref, out_ref):
+    count, comps, width = in_ref.shape
+    groups = rings * pair
+    ring = count // rings
+    sums = []
+    for x in range(rings):
+        part = in_ref[x * ring : (x + 1) * ring].astype(F32).reshape(ring // pair, pair * comps, width)
+        sums.append(jnp.sum(part, axis=0))
+    sums = jnp.concatenate(sums, axis=0)
+    rows = jnp.concatenate([sums[i : i + 1] for comp in range(comps) for i in range(comp, groups * comps, comps)], axis=0)
     row = lax.broadcasted_iota(I32, rows.shape, 0)
     lane = lax.broadcasted_iota(I32, rows.shape, 1)
     zero = (row % groups == 0) & (lane % (width // 2) == 0)
@@ -231,13 +223,13 @@
             out_ref[0, comp : comp + 1, a * 128 : (a + 1) * 128] = total[a : a + 1]
 
 
-def merge_call(groups, ring, green, mechanism, slip, onset, pattern, hypo):
+def merge_call(groups, green, mechanism, slip, onset, pattern, hypo):
     _, comps, kinds, subs, freqs = green.shape
     pats, hypos = slip.shape[0], onset.shape[0]
     lines = 2 * comps * freqs // groups + 16 + pats
     count = pattern.shape[0]
     return pl.pallas_call(
-        lambda *refs: merge_kernel(groups, ring, pats, *refs),
+        lambda *refs: merge_kernel(groups, pats, *refs),
         out_shape=(
             jax.ShapeDtypeStruct((groups, lines, subs), I16),
             jax.ShapeDtypeStruct((count, hypos * pats), BF16),
@@ -252,7 +244,6 @@
             pltpu.VMEM((count,), I32),
             pltpu.VMEM((count,), I32),
             pltpu.VMEM((count, 128), I32),
-            pltpu.VMEM((count, 128), I32),
             pltpu.VMEM((2 * comps, freqs, subs), F32),
             pltpu.SemaphoreType.DMA((2 * comps + 5,)),
         ],
@@ -261,13 +252,13 @@
     )(*(pltpu.with_memory_space_constraint(v, pltpu.HBM) for v in (green, mechanism, slip, onset, pattern, hypo)))
 
 
-def table_call(groups, samples, planes, hypos, pats, msg, pick):
+def table_call(groups, samples, hypos, pats, msg, pick):
     subs = msg.shape[2]
     rows = msg.shape[1] - 16 - pats
     in_vmem = pl.BlockSpec(memory_space=pltpu.VMEM)
     return pl.pallas_call(
         lambda *refs: table_kernel(groups, samples, *refs),
-        out_shape=jax.ShapeDtypeStruct((planes, pick.shape[0] // planes * (rows // 128), 128), BF16),
+        out_shape=jax.ShapeDtypeStruct((pick.shape[0], rows // 128, 128), BF16),
         in_specs=[in_vmem, in_vmem],
         out_specs=in_vmem,
         scratch_shapes=[
@@ -288,35 +279,20 @@
     samples = 2 * freqs
     pats, hypos = slip.shape[0], onset.shape[0]
     groups = lax.axis_size(GROUP)
-    planes = lax.axis_size(PLANE)
-    count = pattern_of_variation.shape[0]
-    rows = 2 * comps * freqs // groups
     params = pltpu.CompilerParams(vmem_limit_bytes=VMEM)
 
-    ring = count // lax.axis_size("x")
-    msg, pick = merge_call(groups, ring, green, mechanism, slip, onset, pattern_of_variation, hypo_of_variation)
+    msg, pick = merge_call(groups, green, mechanism, slip, onset, pattern_of_variation, hypo_of_variation)
     msg = lax.all_to_all(msg, GROUP, 0, 0, tiled=True)
-
-    parts = table_call(groups, samples, planes, hypos, pats, msg, pick)
-
-    parts = lax.all_to_all(parts, PLANE, 0, 0, tiled=True)
-
-    summed = pl.pallas_call(
-        sum_kernel,
-        out_shape=jax.ShapeDtypeStruct((count // planes, rows // 128, 128), F32),
-        compiler_params=params,
-        name="sum",
-    )(parts)
-
-    spectra = lax.all_to_all(summed, GROUP, 0, 0, tiled=True)
+    parts = table_call(groups, samples, hypos, pats, msg, pick)
+    parts = lax.all_to_all(parts, AXES, 0, 0, tiled=True)
 
     tables = [jnp.asarray(t) for t in inverse_tables(groups, freqs, samples)]
     return pl.pallas_call(
-        inverse_kernel,
+        lambda *refs: inverse_kernel(lax.axis_size("x"), lax.axis_size("c"), *refs),
         out_shape=jax.ShapeDtypeStruct((1, comps, samples), F32),
         compiler_params=params,
         name="inverse",
-    )(spectra, *tables)
+    )(parts, *tables)
 
 
 def solution(mesh):

time: 63.3 us -> 61.6 us (0.973)
  blocking collectives: 56.5 us -> 54.6 us
    all_to_all x2 -> x1, blocking collectives: 34.2 us -> 32.3 us  [on_device(): parts = lax.all_to_all(parts, AXES, 0, 0, tiled=True)]
    pallas_call x3 -> x2, Pallas kernels: 3.37 us -> 3.47 us  [the longest x1 2.46 us: merge_call(): pl.pallas_call(lambda *refs: merge_kernel(groups, pats, *refs), out_shape...]
where the time goes in v7:
time: 61.6 us; the launch traced here: 61.4 us
  blocking collectives  54.6 us (89%)
  Pallas kernels  6.79 us (11%)
    all_to_all x1, blocking collectives, on_device(): parts = lax.all_to_all(parts, AXES, 0, 0, tiled=True)  32.3 us
    all_to_all x1, blocking collectives, on_device(): msg = lax.all_to_all(msg, GROUP, 0, 0, tiled=True)  22.3 us
    pallas_call x1, Pallas kernels, table_call(): pl.pallas_call(lambda *refs: table_kernel(groups, samples, *refs), out_sh...  3.32 us
    pallas_call x1, Pallas kernels, merge_call(): pl.pallas_call(lambda *refs: merge_kernel(groups, pats, *refs), out_shape...  2.46 us

profile of v7, /device:TPU:1, one launch (start us, length us, event | category | flops | bytes accessed | tf_op | source)
XLA Modules:
  0.0 61.4 jit_solution(11242923067346880622)
XLA Ops:
  0.0 0.0 copy-start
  0.0 0.0 copy-start.1
  0.0 0.0 copy-start.2
  0.0 2.5 %merge.1 = (s16[8,400,128]{2,1,0:T(8,128)(2,1)S(1)}, bf16[512,1024]{1,0:T(8,128)(2,1)S(1)}) custom-call(bf16[2,2,6,128,512]{4,3,2,1,0:T(8,128)(2,1)} %refs_0_.1, f32[6,128]{1,0:T(8,128)} %refs_1_.2, bf16[128,128]{1,0:T(8,128)(2,1)} %refs_2_.2, s32[8,128]{1,0:T(8,128)} %refs_3_.2, s32[512]{0:T(512)} %refs_4_.1, s32[512]{0:T(512)} %refs_5_.1), custom_call_target="tpu_custom_call" | custom-call | tf_op jit(solution)/shard_map/merge/pallas_call | solution.py:231
  2.5 22.3 %all_to_all.10.refs_0_ = s16[8,400,128]{2,1,0:T(8,128)(2,1)S(1)} all-to-all(s16[8,400,128]{2,1,0:T(8,128)(2,1)S(1)} %get-tuple-element.7), channel_id=1, replica_groups=mesh['x'=4,'zh'=4,'y'=8,'zl'=2,'c'=2] {'x','c'}, dimensions={0} | all-to-all | bytes 1638400 | tf_op jit(solution)/shard_map/all_to_all | solution.py:285
  24.8 3.3 %table.1 = bf16[512,2,128]{2,1,0:T(2,128)(2,1)S(1)} custom-call(s16[8,400,128]{2,1,0:T(8,128)(2,1)S(1)} %all_to_all.10.refs_0_, bf16[512,1024]{1,0:T(8,128)(2,1)S(1)} %get-tuple-element.8.refs_1_), custom_call_target="tpu_custom_call" | custom-call | tf_op jit(solution)/shard_map/table/pallas_call | solution.py:259
  28.1 32.3 %all_to_all.11.refs_0_ = bf16[512,2,128]{2,1,0:T(2,128)(2,1)S(1)} all-to-all(bf16[512,2,128]{2,1,0:T(2,128)(2,1)S(1)} %table.1), channel_id=1, replica_groups=mesh['x'=4,'zh'=4,'y'=8,'zl'=2,'c'=2] {'x','zh','y','zl','c'}, dimensions={0} | all-to-all | bytes 524288 | tf_op jit(solution)/shard_map/all_to_all | solution.py:287
  60.4 0.0 copy-done
  60.4 0.0 copy-done.1
  60.4 0.0 copy-done.2
  60.4 1.0 %inverse.1 = f32[1,2,1024]{2,1,0:T(2,128)} custom-call(bf16[512,2,128]{2,1,0:T(2,128)(2,1)S(1)} %all_to_all.11.refs_0_, bf16[384,256]{1,0:T(8,128)(2,1)S(1)} %copy-done, f32[2,16,128]{2,1,0:T(8,128)S(1)} %copy-done.2, f32[2,8,8,128]{3,2,1,0:T(8,128)S(1)} %copy-done.1), custom_call_target="tpu_custom_call" | custom-call | tf_op jit(solution)/shard_map/inverse/pallas_call | solution.py:290
Async XLA Ops:
  0.0 60.4 %copy-start = (bf16[384,256]{1,0:T(8,128)(2,1)S(1)}, bf16[384,256]{1,0:T(8,128)(2,1)}, u32[]{:S(2)}) copy-start(bf16[384,256]{1,0:T(8,128)(2,1)} %constant.6.clone.refs_1_) | copy-start | bytes 589828
  0.0 60.4 %copy-start.1 = (f32[2,8,8,128]{3,2,1,0:T(8,128)S(1)}, f32[2,8,8,128]{3,2,1,0:T(8,128)}, u32[]{:S(2)}) copy-start(f32[2,8,8,128]{3,2,1,0:T(8,128)} %constant.8.clone.refs_3_) | copy-start | bytes 196612
  0.0 60.4 %copy-start.2 = (f32[2,16,128]{2,1,0:T(8,128)S(1)}, f32[2,16,128]{2,1,0:T(8,128)}, u32[]{:S(2)}) copy-start(f32[2,16,128]{2,1,0:T(8,128)} %constant.7.clone.refs_2_) | copy-start | bytes 49156

commit v8 on v7

--- a/solution.py
+++ b/solution.py
@@ -11,7 +11,8 @@
 from jax.sharding import PartitionSpec as P
 
 AXES = ("x", "zh", "y", "zl", "c")
-GROUP = ("x", "c")
+GROUP = ("c", "x")
+OWNERS = AXES[::-1]
 CODE_TOP = 32000.0
 SLIP_UNIT = 2048.0
 LEAST = 4e-34
@@ -35,19 +36,24 @@
     return c, s
 
 
-def choose(pats, pattern, hypo, pick_ref, across):
+def choose(sizes, pats, pattern, hypo, pick_ref, across, ordered):
     count, entries = pick_ref.shape
     width = min(count, 128)
     for first in range(0, count, width):
         some = slice(first, first + width)
         combo = hypo[some] * pats + pattern[some]
         across[some, :] = jnp.broadcast_to(combo.reshape(1, width), (128, width)).T
+    nx, nh, ny, nl, nc = sizes
+    for x, h, l, c in np.ndindex(nx, nh, nl, nc):
+        source = pl.ds(((x * nh + h) * ny * nl + l) * nc + c, ny, stride=nl * nc)
+        place = pl.ds(((c * nl + l) * ny * nh + h) * nx + x, ny, stride=nh * nx)
+        ordered[place, :] = across[source, :]
     for first in range(0, entries, 128):
         ids = lax.broadcasted_iota(I32, (count, 128), 1) + first
-        pick_ref[:, first : first + 128] = jnp.where(across[...] == ids, 1.0, 0.0).astype(BF16)
-
-
-def merge_kernel(groups, pats, green_ref, mech_ref, slip_ref, onset_ref, pattern_ref, hypo_ref, msg_ref, pick_ref, green, mech, slip, onset, pattern, hypo, across, merged, sems):
+        pick_ref[:, first : first + 128] = jnp.where(ordered[...] == ids, 1.0, 0.0).astype(BF16)
+
+
+def merge_kernel(groups, sizes, pats, green_ref, mech_ref, slip_ref, onset_ref, pattern_ref, hypo_ref, msg_ref, pick_ref, green, mech, slip, onset, pattern, hypo, across, ordered, merged, sems):
     _, comps, kinds, subs, freqs = green_ref.shape
     share = freqs // groups
     end = 2 * comps * share
@@ -65,7 +71,7 @@
         copy.start()
     for copy in rest:
         copy.wait()
-    choose(pats, pattern, hypo, pick_ref, across)
+    choose(sizes, pats, pattern, hypo, pick_ref, across, ordered)
     copies[-2].wait()
     codes = (slip[...].astype(F32) * SLIP_UNIT).astype(I32).astype(I16)
     for g in range(groups):
@@ -223,13 +229,13 @@
             out_ref[0, comp : comp + 1, a * 128 : (a + 1) * 128] = total[a : a + 1]
 
 
-def merge_call(groups, green, mechanism, slip, onset, pattern, hypo):
+def merge_call(groups, sizes, green, mechanism, slip, onset, pattern, hypo):
     _, comps, kinds, subs, freqs = green.shape
     pats, hypos = slip.shape[0], onset.shape[0]
     lines = 2 * comps * freqs // groups + 16 + pats
     count = pattern.shape[0]
     return pl.pallas_call(
-        lambda *refs: merge_kernel(groups, pats, *refs),
+        lambda *refs: merge_kernel(groups, sizes, pats, *refs),
         out_shape=(
             jax.ShapeDtypeStruct((groups, lines, subs), I16),
             jax.ShapeDtypeStruct((count, hypos * pats), BF16),
@@ -243,6 +249,7 @@
             pltpu.VMEM((hypos, subs), I32),
             pltpu.VMEM((count,), I32),
             pltpu.VMEM((count,), I32),
+            pltpu.VMEM((count, 128), I32),
             pltpu.VMEM((count, 128), I32),
             pltpu.VMEM((2 * comps, freqs, subs), F32),
             pltpu.SemaphoreType.DMA((2 * comps + 5,)),
@@ -281,14 +288,15 @@
     groups = lax.axis_size(GROUP)
     params = pltpu.CompilerParams(vmem_limit_bytes=VMEM)
 
-    msg, pick = merge_call(groups, green, mechanism, slip, onset, pattern_of_variation, hypo_of_variation)
+    sizes = tuple(lax.axis_size(axis) for axis in AXES)
+    msg, pick = merge_call(groups, sizes, green, mechanism, slip, onset, pattern_of_variation, hypo_of_variation)
     msg = lax.all_to_all(msg, GROUP, 0, 0, tiled=True)
     parts = table_call(groups, samples, hypos, pats, msg, pick)
-    parts = lax.all_to_all(parts, AXES, 0, 0, tiled=True)
+    parts = lax.all_to_all(parts, OWNERS, 0, 0, tiled=True)
 
     tables = [jnp.asarray(t) for t in inverse_tables(groups, freqs, samples)]
     return pl.pallas_call(
-        lambda *refs: inverse_kernel(lax.axis_size("x"), lax.axis_size("c"), *refs),
+        lambda *refs: inverse_kernel(lax.axis_size("c"), lax.axis_size("x"), *refs),
         out_shape=jax.ShapeDtypeStruct((1, comps, samples), F32),
         compiler_params=params,
         name="inverse",

time: 61.6 us -> 61.5 us (level)
  no operation moved by 1% of the time
where the time goes in v8:
time: 61.5 us; the launch traced here: 61.3 us
  blocking collectives  54.2 us (88%)
  Pallas kernels  7.14 us (12%)
    all_to_all x1, blocking collectives, on_device(): parts = lax.all_to_all(parts, OWNERS, 0, 0, tiled=True)  31.9 us
    all_to_all x1, blocking collectives, on_device(): msg = lax.all_to_all(msg, GROUP, 0, 0, tiled=True)  22.2 us
    pallas_call x1, Pallas kernels, table_call(): pl.pallas_call(lambda *refs: table_kernel(groups, samples, *refs), out_sh...  3.32 us
    pallas_call x1, Pallas kernels, merge_call(): pl.pallas_call(lambda *refs: merge_kernel(groups, sizes, pats, *refs), ou...  2.82 us

profile of v8, /device:TPU:1, one launch (start us, length us, event | category | flops | bytes accessed | tf_op | source)
XLA Modules:
  0.0 61.3 jit_solution(4211134562973628709)
XLA Ops:
  0.0 0.0 copy-start
  0.0 0.0 copy-start.1
  0.0 0.0 copy-start.2
  0.0 2.8 %merge.1 = (s16[8,400,128]{2,1,0:T(8,128)(2,1)S(1)}, bf16[512,1024]{1,0:T(8,128)(2,1)S(1)}) custom-call(bf16[2,2,6,128,512]{4,3,2,1,0:T(8,128)(2,1)} %refs_0_.1, f32[6,128]{1,0:T(8,128)} %refs_1_.2, bf16[128,128]{1,0:T(8,128)(2,1)} %refs_2_.2, s32[8,128]{1,0:T(8,128)} %refs_3_.2, s32[512]{0:T(512)} %refs_4_.1, s32[512]{0:T(512)} %refs_5_.1), custom_call_target="tpu_custom_call" | custom-call | tf_op jit(solution)/shard_map/merge/pallas_call | solution.py:237
  2.8 22.2 %all_to_all.10.refs_0_ = s16[8,400,128]{2,1,0:T(8,128)(2,1)S(1)} all-to-all(s16[8,400,128]{2,1,0:T(8,128)(2,1)S(1)} %get-tuple-element.7), channel_id=1, replica_groups=mesh['x'=4,'zh'=4,'y'=8,'zl'=2,'c'=2] {'c','x'}, dimensions={0} | all-to-all | bytes 1638400 | tf_op jit(solution)/shard_map/all_to_all | solution.py:293
  25.1 3.3 %table.1 = bf16[512,2,128]{2,1,0:T(2,128)(2,1)S(1)} custom-call(s16[8,400,128]{2,1,0:T(8,128)(2,1)S(1)} %all_to_all.10.refs_0_, bf16[512,1024]{1,0:T(8,128)(2,1)S(1)} %get-tuple-element.8.refs_1_), custom_call_target="tpu_custom_call" | custom-call | tf_op jit(solution)/shard_map/table/pallas_call | solution.py:266
  28.4 31.9 %all_to_all.11.refs_0_ = bf16[512,2,128]{2,1,0:T(2,128)(2,1)S(1)} all-to-all(bf16[512,2,128]{2,1,0:T(2,128)(2,1)S(1)} %table.1), channel_id=1, replica_groups=mesh['x'=4,'zh'=4,'y'=8,'zl'=2,'c'=2] {'c','zl','y','zh','x'}, dimensions={0} | all-to-all | bytes 524288 | tf_op jit(solution)/shard_map/all_to_all | solution.py:295
  60.3 0.0 copy-done
  60.3 0.0 copy-done.1
  60.3 0.0 copy-done.2
  60.3 1.0 %inverse.1 = f32[1,2,1024]{2,1,0:T(2,128)} custom-call(bf16[512,2,128]{2,1,0:T(2,128)(2,1)S(1)} %all_to_all.11.refs_0_, bf16[384,256]{1,0:T(8,128)(2,1)S(1)} %copy-done, f32[2,16,128]{2,1,0:T(8,128)S(1)} %copy-done.2, f32[2,8,8,128]{3,2,1,0:T(8,128)S(1)} %copy-done.1), custom_call_target="tpu_custom_call" | custom-call | tf_op jit(solution)/shard_map/inverse/pallas_call | solution.py:298
Async XLA Ops:
  0.0 60.3 %copy-start = (bf16[384,256]{1,0:T(8,128)(2,1)S(1)}, bf16[384,256]{1,0:T(8,128)(2,1)}, u32[]{:S(2)}) copy-start(bf16[384,256]{1,0:T(8,128)(2,1)} %constant.6.clone.refs_1_) | copy-start | bytes 589828
  0.0 60.3 %copy-start.1 = (f32[2,8,8,128]{3,2,1,0:T(8,128)S(1)}, f32[2,8,8,128]{3,2,1,0:T(8,128)}, u32[]{:S(2)}) copy-start(f32[2,8,8,128]{3,2,1,0:T(8,128)} %constant.8.clone.refs_3_) | copy-start | bytes 196612
  0.0 60.3 %copy-start.2 = (f32[2,16,128]{2,1,0:T(8,128)S(1)}, f32[2,16,128]{2,1,0:T(8,128)}, u32[]{:S(2)}) copy-start(f32[2,16,128]{2,1,0:T(8,128)} %constant.7.clone.refs_2_) | copy-start | bytes 49156

commit v9 on v7

--- a/solution.py
+++ b/solution.py
@@ -76,14 +76,15 @@
 
     def merge(i):
         top = jnp.zeros((8, subs), F32)
-        for tile in range(freqs // subs):
-            piece = slice(tile * subs, (tile + 1) * subs)
-            total = cols[0] * green[i, 0, :, piece].astype(F32)
+        for first in range(0, freqs, 2 * subs):
+            piece = slice(first, first + 2 * subs)
+            wide = [jnp.concatenate([col] * 2, axis=1) for col in cols]
+            total = wide[0] * green[i, 0, :, piece].astype(F32)
             for k in range(1, kinds):
-                total = total + cols[k] * green[i, k, :, piece].astype(F32)
+                total = total + wide[k] * green[i, k, :, piece].astype(F32)
             total = total.T
             merged[i, piece, :] = total
-            top = jnp.maximum(top, jnp.max(jnp.abs(total).reshape(subs // 8, 8, subs), axis=0))
+            top = jnp.maximum(top, jnp.max(jnp.abs(total).reshape(-1, 8, subs), axis=0))
         return top
 
     def encode(i, top):
@@ -164,10 +165,9 @@
                         im_out.append(c * im - s * re)
                     real[comp].append(jnp.concatenate(re_out, axis=1).astype(BF16))
                     imag[comp].append(jnp.concatenate(im_out, axis=1).astype(BF16))
-            for comp in range(2):
-                block = jnp.concatenate(real[comp] + imag[comp], axis=1)
-                for src in range(first, first + batch):
-                    shifted[h, src * subs : (src + 1) * subs, comp * 2 * share : (comp + 1) * 2 * share] = block[src - first].T
+            for src in range(first, first + batch):
+                block = jnp.concatenate([part[src - first] for comp in range(2) for part in real[comp] + imag[comp]], axis=0)
+                shifted[h, src * subs : (src + 1) * subs, :] = block.T
         sums = jnp.dot(slips[...], shifted[h], preferred_element_type=F32)
         sums = sums.astype(BF16)
         table[h * pats : (h + 1) * pats, :] = sums

time: 61.6 us -> 61.1 us (level)
  no operation moved by 1% of the time
where the time goes in v9:
time: 61.1 us; the launch traced here: 61 us
  blocking collectives  54.6 us (89%)
  Pallas kernels  6.34 us (10%)
    all_to_all x1, blocking collectives, on_device(): parts = lax.all_to_all(parts, AXES, 0, 0, tiled=True)  32.3 us
    all_to_all x1, blocking collectives, on_device(): msg = lax.all_to_all(msg, GROUP, 0, 0, tiled=True)  22.3 us
    pallas_call x1, Pallas kernels, table_call(): pl.pallas_call(lambda *refs: table_kernel(groups, samples, *refs), out_sh...  2.86 us
    pallas_call x1, Pallas kernels, merge_call(): pl.pallas_call(lambda *refs: merge_kernel(groups, pats, *refs), out_shape...  2.46 us

profile of v9, /device:TPU:1, one launch (start us, length us, event | category | flops | bytes accessed | tf_op | source)
XLA Modules:
  0.0 61.0 jit_solution(3650587665222584977)
XLA Ops:
  0.0 0.0 copy-start
  0.0 0.0 copy-start.1
  0.0 0.0 copy-start.2
  0.0 2.5 %merge.1 = (s16[8,400,128]{2,1,0:T(8,128)(2,1)S(1)}, bf16[512,1024]{1,0:T(8,128)(2,1)S(1)}) custom-call(bf16[2,2,6,128,512]{4,3,2,1,0:T(8,128)(2,1)} %refs_0_.1, f32[6,128]{1,0:T(8,128)} %refs_1_.2, bf16[128,128]{1,0:T(8,128)(2,1)} %refs_2_.2, s32[8,128]{1,0:T(8,128)} %refs_3_.2, s32[512]{0:T(512)} %refs_4_.1, s32[512]{0:T(512)} %refs_5_.1), custom_call_target="tpu_custom_call" | custom-call | tf_op jit(solution)/shard_map/merge/pallas_call | solution.py:231
  2.5 22.3 %all_to_all.10.refs_0_ = s16[8,400,128]{2,1,0:T(8,128)(2,1)S(1)} all-to-all(s16[8,400,128]{2,1,0:T(8,128)(2,1)S(1)} %get-tuple-element.7), channel_id=1, replica_groups=mesh['x'=4,'zh'=4,'y'=8,'zl'=2,'c'=2] {'x','c'}, dimensions={0} | all-to-all | bytes 1638400 | tf_op jit(solution)/shard_map/all_to_all | solution.py:285
  24.8 2.9 %table.1 = bf16[512,2,128]{2,1,0:T(2,128)(2,1)S(1)} custom-call(s16[8,400,128]{2,1,0:T(8,128)(2,1)S(1)} %all_to_all.10.refs_0_, bf16[512,1024]{1,0:T(8,128)(2,1)S(1)} %get-tuple-element.8.refs_1_), custom_call_target="tpu_custom_call" | custom-call | tf_op jit(solution)/shard_map/table/pallas_call | solution.py:259
  27.6 32.3 %all_to_all.11.refs_0_ = bf16[512,2,128]{2,1,0:T(2,128)(2,1)S(1)} all-to-all(bf16[512,2,128]{2,1,0:T(2,128)(2,1)S(1)} %table.1), channel_id=1, replica_groups=mesh['x'=4,'zh'=4,'y'=8,'zl'=2,'c'=2] {'x','zh','y','zl','c'}, dimensions={0} | all-to-all | bytes 524288 | tf_op jit(solution)/shard_map/all_to_all | solution.py:287
  59.9 0.0 copy-done
  60.0 0.0 copy-done.1
  60.0 0.0 copy-done.2
  60.0 1.0 %inverse.1 = f32[1,2,1024]{2,1,0:T(2,128)} custom-call(bf16[512,2,128]{2,1,0:T(2,128)(2,1)S(1)} %all_to_all.11.refs_0_, bf16[384,256]{1,0:T(8,128)(2,1)S(1)} %copy-done, f32[2,16,128]{2,1,0:T(8,128)S(1)} %copy-done.2, f32[2,8,8,128]{3,2,1,0:T(8,128)S(1)} %copy-done.1), custom_call_target="tpu_custom_call" | custom-call | tf_op jit(solution)/shard_map/inverse/pallas_call | solution.py:290
Async XLA Ops:
  0.0 60.0 %copy-start = (bf16[384,256]{1,0:T(8,128)(2,1)S(1)}, bf16[384,256]{1,0:T(8,128)(2,1)}, u32[]{:S(2)}) copy-start(bf16[384,256]{1,0:T(8,128)(2,1)} %constant.6.clone.refs_1_) | copy-start | bytes 589828
  0.0 60.0 %copy-start.1 = (f32[2,8,8,128]{3,2,1,0:T(8,128)S(1)}, f32[2,8,8,128]{3,2,1,0:T(8,128)}, u32[]{:S(2)}) copy-start(f32[2,8,8,128]{3,2,1,0:T(8,128)} %constant.8.clone.refs_3_) | copy-start | bytes 196612
  0.0 60.0 %copy-start.2 = (f32[2,16,128]{2,1,0:T(8,128)S(1)}, f32[2,16,128]{2,1,0:T(8,128)}, u32[]{:S(2)}) copy-start(f32[2,16,128]{2,1,0:T(8,128)} %constant.7.clone.refs_2_) | copy-start | bytes 49156
